TPU v7x, 512 devices: a whole 4x4x16 slice. The times are simulated.
512 devices in a mesh: animals: 128 (over z, x, core), snps: 4 (over y).
Axes of the slice: x: 4, y: 4, z: 16, core: 2. Of those that a mesh axis runs over, the one named last changes fastest.
Arguments:
- animal_rhs: float32 [4, 131072], P(None, 'animals'), may hold values from -6 to 6
- marker_rhs: float32 [4, 25088], P(None, 'snps'), may hold values from -6 to 6
- animal_diagonal: float32 [131072], P('animals'), may hold values from 0.5 to 4
- marker_diagonal: float32 [25088], P('snps'), may hold values from 0.5 to 4
- marker_scale: float32 [25088], P('snps'), may hold values from 0.0031567267 to 0.012626907
- genotypes: bfloat16 [8192, 25088], P('animals', 'snps'), may hold values from -1 to 1, as said below
- tile_weights: bfloat16 [14336, 128, 128], P('animals'), may hold values from -0.375 to 0.375
- tile_rows: int32 [14336], P('animals'), may hold values from 0 to 7
- tile_owner: int32 [14336, 1], P('animals'), may hold values from 0 to 127; in each aligned block of 112 rows (0 to 111, 112 to 223, ...) at most 2 rows name the same one
- tile_local: int32 [14336], P('animals'), may hold values from 0 to 7
- tile_count: int32 [128], P('animals'), may hold values from 98 to 112, as said below
- genotyped_block: int32 [128], P('animals'), may hold values from 0 to 7
Outputs:
- animal_solution: float32 [4, 131072], P(None, 'animals')
- marker_solution: float32 [4, 25088], P(None, 'snps')
- animal_residual: float32 [4, 131072], P(None, 'animals')
- marker_residual: float32 [4, 25088], P(None, 'snps')
Inputs may be any that keep to these rules, and one draw needn't show every extreme that they name: `genotypes`: centred genotype codes, each -1, 0 or 1. `tile_owner`: in the rows of one index of animals (aligned blocks of 112 rows) no owner appears more than 2 times. `tile_count`: some index of animals has all 112 slots live.
All inputs are finite; a program needn't handle non-finite values.
Results may differ from a plain program's by a relative error of at most 0.035.
Values may be sent and summed in bfloat16 or wider, within the bound.
A program may use at most 64 MiB of HBM per device.

v0:
```python
import jax
import jax.numpy as jnp
from jax import lax
from jax.sharding import PartitionSpec as P

ITERS = 3


def body(
    animal_rhs,
    marker_rhs,
    animal_diagonal,
    marker_diagonal,
    marker_scale,
    genotypes,
    tile_weights,
    tile_rows,
    tile_owner,
    tile_local,
    tile_count,
    genotyped_block,
):
    traits, local_animals = animal_rhs.shape
    block_size = tile_weights.shape[1]
    local_blocks = local_animals // block_size
    geno_local = genotypes.shape[0]
    tiles = tile_weights.shape[0]
    group_size = lax.axis_size("animals")
    marker_group = lax.axis_size("snps")
    capacity = max(2, 2 * tiles // group_size)
    highest = lax.Precision.HIGHEST
    slot_ids = jnp.arange(tiles, dtype=jnp.int32)
    live_mask = slot_ids < tile_count[0]
    owners = tile_owner[:, 0]
    earlier = (owners[:, None] == owners[None, :]) & (slot_ids[None, :] < slot_ids[:, None])
    slot_rank = jnp.sum(earlier.astype(jnp.int32), axis=1)
    slot_index = owners * capacity + slot_rank
    placed = (
        slot_index[:, None] == jnp.arange(group_size * capacity, dtype=jnp.int32)[None, :]
    ) & live_mask[:, None]
    requests = jnp.sum(jnp.where(placed, tile_local[:, None] + 1, 0), axis=0) - 1
    asked_ids = lax.all_to_all(
        requests.reshape(group_size, capacity), "animals", split_axis=0, concat_axis=0, tiled=True
    )
    asked_ids = asked_ids.reshape(group_size * capacity)
    served_hot = asked_ids[:, None] == jnp.arange(local_blocks, dtype=jnp.int32)[None, :]
    served_half = served_hot.astype(jnp.bfloat16)
    served_full = served_hot.astype(jnp.float32)
    placed_half = placed.astype(jnp.bfloat16)
    placed_full = placed.astype(jnp.float32)
    row_hot = (
        tile_rows[None, :] == jnp.arange(local_blocks, dtype=jnp.int32)[:, None]
    ) & live_mask[None, :]
    row_full = row_hot.astype(jnp.float32)
    row_half = row_hot.astype(jnp.bfloat16)
    geno_hot = (jnp.arange(local_blocks, dtype=jnp.int32) == genotyped_block[0]).astype(jnp.float32)

    def local_inner(first_u, first_m, second_u, second_m):
        return (
            jnp.sum(first_u * second_u, axis=1) / marker_group
            + jnp.sum(first_m * second_m, axis=1) / group_size
        )

    def norm_sum(first_u, first_m, second_u, second_m):
        return lax.psum(local_inner(first_u, first_m, second_u, second_m), ("animals", "snps"))

    animal_guess = jnp.zeros_like(animal_rhs)
    marker_guess = jnp.zeros_like(marker_rhs)
    animal_residual = animal_rhs
    marker_residual = marker_rhs
    animal_precond = animal_residual / animal_diagonal
    marker_precond = marker_residual / marker_diagonal
    animal_search = animal_precond
    marker_search = marker_precond
    rho_now = norm_sum(animal_residual, marker_residual, animal_precond, marker_precond)
    for iteration in range(ITERS):
        blocks = animal_search.astype(jnp.bfloat16).reshape(traits, local_blocks, block_size)
        blocks = jnp.transpose(blocks, (1, 0, 2)).reshape(local_blocks, traits * block_size)
        served = jnp.dot(served_half, blocks, preferred_element_type=jnp.float32).astype(
            jnp.bfloat16
        )
        arrived = lax.all_to_all(
            served.reshape(group_size, capacity, traits * block_size),
            "animals",
            split_axis=0,
            concat_axis=0,
            tiled=True,
        )
        arrived = arrived.reshape(group_size * capacity, traits * block_size)
        fetched = jnp.dot(placed_half, arrived, preferred_element_type=jnp.float32).astype(
            jnp.bfloat16
        )
        fetched = fetched.reshape(tiles, traits, block_size)
        products = jnp.einsum(
            "tik,tsk->tsi", tile_weights, fetched, preferred_element_type=jnp.float32
        )
        row_sums = jnp.dot(
            row_full, products.reshape(tiles, traits * block_size), precision=highest
        ).astype(jnp.bfloat16)
        per_tile = jnp.dot(row_half.T, row_sums, preferred_element_type=jnp.float32).astype(
            jnp.bfloat16
        )
        per_tile = per_tile.reshape(tiles, traits, block_size)
        back_terms = jnp.einsum(
            "tik,tsi->tsk", tile_weights, per_tile, preferred_element_type=jnp.float32
        )
        outgoing = jnp.dot(
            placed_full.T, back_terms.reshape(tiles, traits * block_size), precision=highest
        )
        returned = lax.all_to_all(
            outgoing.reshape(group_size, capacity, traits * block_size).astype(jnp.bfloat16),
            "animals",
            split_axis=0,
            concat_axis=0,
            tiled=True,
        ).astype(jnp.float32)
        gathered = jnp.dot(
            served_full.T,
            returned.reshape(group_size * capacity, traits * block_size),
            precision=highest,
        )
        ped_terms = jnp.transpose(
            gathered.reshape(local_blocks, traits, block_size), (1, 0, 2)
        ).reshape(traits, local_animals)
        whole = animal_search.reshape(traits, local_blocks, block_size)
        own_rows = jnp.sum(whole * geno_hot[None, :, None], axis=1)[:, :geno_local]
        scaled = (marker_search * marker_scale).astype(jnp.bfloat16)
        partial_value = lax.dot_general(
            scaled, genotypes, (((1,), (1,)), ((), ())), preferred_element_type=jnp.float32
        )
        geno_sum = own_rows + lax.psum(partial_value, "snps")
        geno_half = geno_sum.astype(jnp.bfloat16)
        marker_part = jnp.dot(geno_half, genotypes, preferred_element_type=jnp.float32)
        marker_back = lax.psum(marker_part, "animals")
        padded_geno = jnp.pad(geno_sum, ((0, 0), (0, block_size - geno_local)))
        spread_geno = (geno_hot[None, :, None] * padded_geno[:, None, :]).reshape(
            traits, local_animals
        )
        animal_out = animal_diagonal * animal_search + ped_terms + spread_geno
        marker_out = marker_diagonal * marker_search + marker_scale * marker_back
        curvature = lax.psum(
            local_inner(animal_search, marker_search, animal_out, marker_out), ("animals", "snps")
        )
        step_size = rho_now / curvature
        animal_guess = animal_guess + step_size[:, None] * animal_search
        marker_guess = marker_guess + step_size[:, None] * marker_search
        animal_residual = animal_residual - step_size[:, None] * animal_out
        marker_residual = marker_residual - step_size[:, None] * marker_out
        if iteration + 1 < ITERS:
            animal_precond = animal_residual / animal_diagonal
            marker_precond = marker_residual / marker_diagonal
            rho_next = norm_sum(animal_residual, marker_residual, animal_precond, marker_precond)
            beta_ratio = rho_next / rho_now
            animal_search = animal_precond + beta_ratio[:, None] * animal_search
            marker_search = marker_precond + beta_ratio[:, None] * marker_search
            rho_now = rho_next
    return (animal_guess, marker_guess, animal_residual, marker_residual)


def solution(mesh):
    placed = (
        P(None, "animals"),
        P(None, "snps"),
        P("animals"),
        P("snps"),
        P("snps"),
        P("animals", "snps"),
        P("animals", None, None),
        P("animals"),
        P("animals", None),
        P("animals"),
        P("animals"),
        P("animals"),
    )
    return jax.shard_map(
        body,
        mesh=mesh,
        in_specs=placed,
        out_specs=(P(None, "animals"), P(None, "snps"), P(None, "animals"), P(None, "snps")),
        check_vma=False,
    )
```

profile of v0, /device:TPU:1, one launch (start us, length us, event | category | flops | bytes accessed | tf_op | source)
XLA Modules:
  0.0 1676.5 jit_solution(3082154694706076422)
XLA Ops:
  11.1 20.4 %all-to-all-start = ((s32[128,1,2]{2,1,0:T(1,128)}), s32[128,1,2]{2,1,0:T(1,128)S(1)}, u32[]{:S(2)}, u32[]{:S(2)}) async-start(s32[128,1,2]{2,1,0:T(1,128)} %bitcast.4), calls=%async_computation | async-start | bytes 131072 | tf_op jit(solution)/shard_map/all_to_all | solution.py:42
  32.2 14.1 all-to-all-done
  48.8 5.7 all-to-all-start.1
  56.4 9.3 psum.85
  65.8 9.3 all-to-all-done.1
  84.7 8.4 all-to-all-start.2
  94.2 318.5 %all-reduce.8.cloned.1.call-done = f32[4,6272]{1,0:T(4,128)} async-done(((f32[4,6272]{1,0:T(4,128)}), f32[4,6272]{1,0:T(4,128)}) %all-reduce.8.cloned.1.call-update) | async-done | bytes 100368 | tf_op jit(solution)/shard_map/psum | solution.py:134
  414.5 101.6 %all-reduce.3 = (f32[4]{0:T(128)S(1)}, f32[4]{0:T(128)S(1)}) all-reduce(f32[4]{0:T(128)S(1)} %get-tuple-element.29, f32[4]{0:T(128)S(1)} %get-tuple-element.28), channel_id=1, replica_groups=mesh['animals'=128,'snps'=4] {'animals','snps'}, use_global_device_ids=true, to_apply=%region_2.3 | all-reduce | flops 8 | bytes 64 | tf_op jit(solution)/shard_map/psum | solution.py:65
  517.4 99.1 %psum.88 = f32[4]{0:T(128)S(1)} all-reduce(f32[4]{0:T(128)S(1)} %multiply_add_fusion.13), channel_id=1, replica_groups=mesh['animals'=128,'snps'=4] {'animals','snps'}, use_global_device_ids=true, to_apply=%region_13.14 | all-reduce | flops 4 | bytes 32 | tf_op jit(solution)/shard_map/psum | solution.py:65
  617.7 9.8 all-to-all-start.3
  627.7 20.4 %all-to-all-done.3 = bf16[128,2,512]{2,1,0:T(2,128)(2,1)S(1)} async-done(((bf16[128,2,512]{2,1,0:T(2,128)(2,1)}), bf16[128,2,512]{2,1,0:T(2,128)(2,1)S(1)}, u32[]{:S(2)}, u32[]{:S(2)}) %all-to-all-start.3) | async-done | bytes 262176 | tf_op jit(solution)/shard_map/all_to_all | solution.py:82
  648.4 4.0 fusion.80
  657.6 8.3 all-to-all-start.4
  666.3 7.2 psum.89
  674.4 314.2 %all-reduce.10.cloned.1.call-done = f32[4,6272]{1,0:T(4,128)} async-done(((f32[4,6272]{1,0:T(4,128)}), f32[4,6272]{1,0:T(4,128)}) %all-reduce.10.cloned.1.call-update) | async-done | bytes 100368 | tf_op jit(solution)/shard_map/psum | solution.py:134
  990.3 101.6 %psum.91 = f32[4]{0:T(128)S(1)} all-reduce(f32[4]{0:T(128)S(1)} %multiply_add_fusion.12), channel_id=1, replica_groups=mesh['animals'=128,'snps'=4] {'animals','snps'}, use_global_device_ids=true, to_apply=%region_19.20 | all-reduce | flops 4 | bytes 32 | tf_op jit(solution)/shard_map/psum | solution.py:141
  1093.3 99.0 %psum.92 = f32[4]{0:T(128)S(1)} all-reduce(f32[4]{0:T(128)S(1)} %multiply_add_fusion.11), channel_id=1, replica_groups=mesh['animals'=128,'snps'=4] {'animals','snps'}, use_global_device_ids=true, to_apply=%region_22.23 | all-reduce | flops 4 | bytes 32 | tf_op jit(solution)/shard_map/psum | solution.py:65
  1193.4 9.9 all-to-all-start.5
  1203.3 20.4 %all-to-all-done.5 = bf16[128,2,512]{2,1,0:T(2,128)(2,1)S(1)} async-done(((bf16[128,2,512]{2,1,0:T(2,128)(2,1)}), bf16[128,2,512]{2,1,0:T(2,128)(2,1)S(1)}, u32[]{:S(2)}, u32[]{:S(2)}) %all-to-all-start.5) | async-done | bytes 262176 | tf_op jit(solution)/shard_map/all_to_all | solution.py:82
  1224.1 4.0 fusion.82
  1233.3 8.3 all-to-all-start.6
  1241.9 7.2 psum.93
  1250.1 314.2 %all-reduce.12.cloned.1.call-done = f32[4,6272]{1,0:T(4,128)} async-done(((f32[4,6272]{1,0:T(4,128)}), f32[4,6272]{1,0:T(4,128)}) %all-reduce.12.cloned.1.call-update) | async-done | bytes 100368 | tf_op jit(solution)/shard_map/psum | solution.py:134
  1566.0 101.6 %psum.95 = f32[4]{0:T(128)S(1)} all-reduce(f32[4]{0:T(128)S(1)} %multiply_add_fusion.10), channel_id=1, replica_groups=mesh['animals'=128,'snps'=4] {'animals','snps'}, use_global_device_ids=true, to_apply=%region_28.29 | all-reduce | flops 4 | bytes 32 | tf_op jit(solution)/shard_map/psum | solution.py:141
  (127 shorter events, 44.4 us)
Async XLA Ops:
  7.2 48.0 %copy-start = (bf16[64,6272]{1,0:T(8,128)(2,1)S(1)}, bf16[64,6272]{1,0:T(8,128)(2,1)}, u32[]{:S(2)}) copy-start(bf16[64,6272]{1,0:T(8,128)(2,1)} %param.17) | copy-start | bytes 2408452
  11.1 35.2 %all-to-all-start = ((s32[128,1,2]{2,1,0:T(1,128)}), s32[128,1,2]{2,1,0:T(1,128)S(1)}, u32[]{:S(2)}, u32[]{:S(2)}) async-start(s32[128,1,2]{2,1,0:T(1,128)} %bitcast.4), calls=%async_computation | async-start | bytes 131072 | tf_op jit(solution)/shard_map/all_to_all | solution.py:42
  48.0 31.5 %copy-start.6 = (s32[112]{0:T(128)S(1)}, s32[112]{0:T(128)}, u32[]{:S(2)}) copy-start(s32[112]{0:T(128)} %param.19) | copy-start | bytes 1348
  48.8 26.3 %all-to-all-start.1 = ((bf16[128,2,512]{2,1,0:T(2,128)(2,1)}), bf16[128,2,512]{2,1,0:T(2,128)(2,1)S(1)}, u32[]{:S(2)}, u32[]{:S(2)}) async-start(bf16[128,2,512]{2,1,0:T(2,128)(2,1)} %reshape.201), calls=%async_computation.1 | async-start | bytes 524288 | tf_op jit(solution)/shard_map/all_to_all | solution.py:82
  80.0 332.8 %copy-start.1 = (f32[6272]{0:T(1024)S(1)}, f32[6272]{0:T(1024)}, u32[]{:S(2)}) copy-start(f32[6272]{0:T(1024)} %param.15) | copy-start | bytes 75268
  80.0 332.7 %copy-start.2 = (f32[6272]{0:T(1024)S(1)}, f32[6272]{0:T(1024)}, u32[]{:S(2)}) copy-start(f32[6272]{0:T(1024)} %param.16) | copy-start | bytes 75268
  80.0 332.7 %copy-start.3 = (f32[4,6272]{1,0:T(4,128)S(1)}, f32[4,6272]{1,0:T(4,128)}, u32[]{:S(2)}) copy-start(f32[4,6272]{1,0:T(4,128)} %param.13) | copy-start | bytes 301060
  80.0 334.2 %copy-start.4 = (f32[4,1024]{1,0:T(4,128)S(1)}, f32[4,1024]{1,0:T(4,128)}, u32[]{:S(2)}) copy-start(f32[4,1024]{1,0:T(4,128)} %param.12) | copy-start | bytes 49156
  80.1 334.2 %copy-start.5 = (f32[1024]{0:T(1024)S(1)}, f32[1024]{0:T(1024)}, u32[]{:S(2)}) copy-start(f32[1024]{0:T(1024)} %param.14) | copy-start | bytes 12292
  84.7 329.1 %all-to-all-start.2 = ((bf16[128,2,512]{2,1,0:T(2,128)(2,1)}), bf16[128,2,512]{2,1,0:T(2,128)(2,1)S(1)}, u32[]{:S(2)}, u32[]{:S(2)}) async-start(bf16[128,2,512]{2,1,0:T(2,128)(2,1)} %copy.30), calls=%async_computation.2 | async-start | bytes 524288 | tf_op jit(solution)/shard_map/all_to_all | solution.py:110
  93.1 319.6 %all-reduce.8.cloned.1.call-start = ((), (), s32[]{:S(2)}) async-start(), calls=%async_computation.7 | async-start | bytes 200704 | tf_op jit(solution)/shard_map/psum | solution.py:134
  617.7 30.3 %all-to-all-start.3 = ((bf16[128,2,512]{2,1,0:T(2,128)(2,1)}), bf16[128,2,512]{2,1,0:T(2,128)(2,1)S(1)}, u32[]{:S(2)}, u32[]{:S(2)}) async-start(bf16[128,2,512]{2,1,0:T(2,128)(2,1)} %reshape.212), calls=%async_computation.3 | async-start | bytes 524288 | tf_op jit(solution)/shard_map/all_to_all | solution.py:82
  657.6 332.1 %all-to-all-start.4 = ((bf16[128,2,512]{2,1,0:T(2,128)(2,1)}), bf16[128,2,512]{2,1,0:T(2,128)(2,1)S(1)}, u32[]{:S(2)}, u32[]{:S(2)}) async-start(bf16[128,2,512]{2,1,0:T(2,128)(2,1)} %copy.32), calls=%async_computation.4 | async-start | bytes 524288 | tf_op jit(solution)/shard_map/all_to_all | solution.py:110
  665.9 322.7 %all-reduce.10.cloned.1.call-start = ((), (), s32[]{:S(2)}) async-start(), calls=%async_computation.8 | async-start | bytes 200704 | tf_op jit(solution)/shard_map/psum | solution.py:134
  1193.4 30.3 %all-to-all-start.5 = ((bf16[128,2,512]{2,1,0:T(2,128)(2,1)}), bf16[128,2,512]{2,1,0:T(2,128)(2,1)S(1)}, u32[]{:S(2)}, u32[]{:S(2)}) async-start(bf16[128,2,512]{2,1,0:T(2,128)(2,1)} %reshape.223), calls=%async_computation.5 | async-start | bytes 524288 | tf_op jit(solution)/shard_map/all_to_all | solution.py:82
  1233.3 332.1 %all-to-all-start.6 = ((bf16[128,2,512]{2,1,0:T(2,128)(2,1)}), bf16[128,2,512]{2,1,0:T(2,128)(2,1)S(1)}, u32[]{:S(2)}, u32[]{:S(2)}) async-start(bf16[128,2,512]{2,1,0:T(2,128)(2,1)} %copy.34), calls=%async_computation.6 | async-start | bytes 524288 | tf_op jit(solution)/shard_map/all_to_all | solution.py:110
  1241.6 322.7 %all-reduce.12.cloned.1.call-start = ((), (), s32[]{:S(2)}) async-start(), calls=%async_computation.9 | async-start | bytes 200704 | tf_op jit(solution)/shard_map/psum | solution.py:134
Sparse Core Ops, SparseCore 0:
  98.0 314.6 all-reduce.7
  674.6 314.0 all-reduce.9
  1250.2 314.0 all-reduce.11
where the time goes:
time: 1680 us
  waiting for transfers between devices  1010 us (60%)
  blocking collectives  527 us (31%)
  starting transfers between devices  70.9 us (4%)
  matrix products  30.5 us (2%)
    psum x3, waiting for transfers between devices, body(): marker_back = lax.psum(marker_part, 'animals')  947 us
    psum x3, blocking collectives, norm_sum(): lax.psum(local_inner(first_u, first_m, second_u, second_m), ('animals', '...  300 us
    psum x2, blocking collectives, body(): lax.psum(local_inner(animal_search, marker_search, animal_out, marker_out...  203 us
    all_to_all x3, waiting for transfers between devices, body(): lax.all_to_all(served.reshape(group_size, capacity, traits * block_size),...  50.1 us
  transfers between devices with their start and end apart: 10, of which 7 were waited for; matrix products, arithmetic and copies ran while one was open for 1% of the time, Pallas kernels for 0%

commit v1 on v0

v1 whole, which is shorter than its diff:
```python
from types import SimpleNamespace

import jax
import jax.numpy as jnp
from jax import lax
from jax.experimental import pallas as pl
from jax.experimental.pallas import tpu as pltpu
from jax.sharding import PartitionSpec as P

ITERS = 3
CAP = 2
NJ = 8
JB, ZB, ZS = 7, 7, 2
LANES = 128
A1, A2, B1, B2, Y, R1, R2, G1, G2, STAGES = range(10)
SZ, SX, SY, STEPS = range(4)
SUMS = 2 * ITERS - 1
ANIMALS, SNPS = "animals", "snps"
MESH = pl.DeviceIdType.MESH
F32, BF16, I32 = jnp.float32, jnp.bfloat16, jnp.int32


def iota(shape, dim):
    return lax.broadcasted_iota(I32, shape, dim)


def total(x):
    return jnp.sum(jnp.sum(x, axis=1, keepdims=True), axis=0, keepdims=True)


def kernel(nz, ny, arhs_h, mrhs_h, adiag_h, mdiag_h, mscale_h, geno_h, w_h, rows_h, owner_h, local_h, count_s,
           gblk_s, asol, msol, ares, mres, s):
    traits, markers = mrhs_h.shape
    tiles = w_h.shape[0]
    nb = adiag_h.shape[0]
    geno = geno_h.shape[0]
    slots = nz * CAP
    all_slots, dense = NJ * slots, nz * nb
    wide = ZB * LANES
    me, y = lax.axis_index(ANIMALS), lax.axis_index(SNPS)
    z, j = lax.div(me, NJ), lax.rem(me, NJ)
    in_jb = j < JB
    in_zb = (lax.rem(z, ZS) == 0) & (z < ZB * ZS)

    def to_z(zz):
        return {ANIMALS: zz * NJ + j, SNPS: y}

    def to_j(jj):
        return {ANIMALS: z * NJ + jj, SNPS: y}

    def to_y(yy):
        return {ANIMALS: me, SNPS: yy}

    def each(here, count, act):
        half = count // 2
        act(lax.rem(here + half, count))

        def step(d, c):
            act(lax.rem(here + half - d, count))
            act(lax.rem(here + half + d, count))
            return c

        lax.fori_loop(1, half, step, 0)

    def push(src, dst, send, recv, device):
        pltpu.make_async_remote_copy(src_ref=src, dst_ref=dst, send_sem=send, recv_sem=recv,
                                     device_id=device, device_id_type=MESH).start()

    def await_bytes(ref, sem):
        pltpu.make_async_copy(ref, ref, sem).wait()

    barrier = pltpu.get_barrier_semaphore()

    def greet(device):
        pl.semaphore_signal(barrier, inc=1, device_id=device, device_id_type=MESH)

    each(z, nz, lambda zz: greet(to_z(zz)))
    each(j, NJ, lambda jj: greet(to_j(jj)))
    each(y, ny, lambda yy: greet(to_y(yy)))

    pairs = ((arhs_h, s.arhs), (adiag_h, s.adiag), (mrhs_h, s.mrhs), (mdiag_h, s.mdiag.at[0]), (mscale_h, s.mscale.at[0]),
             (owner_h, s.owner), (local_h, s.local), (rows_h, s.rows), (geno_h, s.g), (w_h, s.w))
    gets = [pltpu.make_async_copy(src, dst, s.get.at[k]) for k, (src, dst) in enumerate(pairs)]
    for get in gets:
        get.start()
    gets[0].wait()
    gets[1].wait()

    blk = iota((nb, LANES), 0)
    lane = iota((nb, LANES), 1)
    sub = iota((8, LANES), 0)
    trait_col = iota((traits, 1), 0)
    lane4 = iota((traits, LANES), 1)
    a_diag = s.adiag[...]
    a_inv = 1.0 / a_diag
    r_a = jnp.zeros((nb, LANES), F32)
    for k in range(nb):
        row = jnp.where(trait_col == y, s.arhs[:, k * LANES:(k + 1) * LANES], 0.0)
        r_a = jnp.where(blk == k, jnp.sum(row, axis=0, keepdims=True), r_a)
    z_a = r_a * a_inv
    sol_a = jnp.zeros((nb, LANES), F32)
    gblk = gblk_s[0]
    cuts = [slice(b * wide, (b + 1) * wide) for b in range(JB)]
    col = jnp.zeros((traits, 1), F32)

    def plan():
        own = s.owner[...]
        names = (iota((nz * NJ, tiles), 0) == own).astype(F32)
        before = (iota((tiles, tiles), 0) < iota((tiles, tiles), 1)).astype(F32)
        earlier = jnp.dot(names.astype(BF16), before.astype(BF16), preferred_element_type=F32)
        rank = jnp.sum(names * earlier, axis=0, keepdims=True)
        slot = (lax.rem(own, NJ) * slots + lax.div(own, NJ) * CAP).astype(F32) + rank
        slot = jnp.where(iota((1, tiles), 1) < count_s[0], slot, -1.0)
        hit = (iota((all_slots, tiles), 0).astype(F32) == slot).astype(F32)
        asked = jnp.sum(hit * (s.local[...] + 1).astype(F32), axis=1, keepdims=True)
        asked = jnp.broadcast_to(asked, (all_slots, LANES))
        s.id_send[...] = asked.reshape(NJ, slots, LANES).astype(BF16)
        each(j, NJ, lambda jj: push(s.id_send.at[jj], s.id_recv.at[j], s.once_send.at[0], s.once_recv.at[0], to_j(jj)))
        s.id_recv[j] = s.id_send[j]
        s.table[...] = jnp.zeros_like(s.table)
        s.table[:, :tiles] = hit
        table = s.table[...]
        s.placed_t[...] = table.astype(BF16)
        s.placed[...] = table.T.astype(BF16)
        s.back[...] = jnp.zeros_like(s.back)

    def serve():
        await_bytes(s.id_recv.at[pl.ds(0, NJ - 1)], s.once_recv.at[0])
        ids = s.id_recv[...].astype(F32).reshape(all_slots, LANES)[:, :dense]
        source = lax.div(lax.rem(iota((all_slots, dense), 0), slots), CAP) * nb
        named = iota((all_slots, dense), 1).astype(F32) == source.astype(F32) + ids - 1.0
        pmat = ((ids > 0.5) & named).astype(F32)
        s.pmat[...] = pmat.astype(BF16)
        s.pmat_t[...] = pmat.T.astype(BF16)

    pl.semaphore_wait(barrier, nz + NJ + ny - 3)

    def start(it, stage, src, dst, device):
        push(src, dst, s.send.at[it, stage], s.recv.at[it, stage], device)

    def arrived(it, stage, ref):
        await_bytes(ref, s.recv.at[it, stage])

    def scalar_push(n, step, src, dst, device):
        push(src, dst, s.sum_send.at[n, step], s.sum_recv.at[n, step], device)

    def scalar_z(n, parts):
        row = jnp.zeros((1, LANES), F32)
        for k, part in enumerate(parts):
            row = jnp.where(lane4[:1] == k, total(part), row)
        s.sz_send[n] = row
        s.sz_recv[n, z] = row
        each(z, nz, lambda zz: scalar_push(n, SZ, s.sz_send.at[n], s.sz_recv.at[n, z], to_z(zz)))

    def scalar_x(n):
        await_bytes(s.sz_recv.at[n, pl.ds(0, nz - 1)], s.sum_recv.at[n, SZ])
        row = jnp.sum(s.sz_recv[n], axis=0)
        s.sx_send[n] = row
        s.sx_recv[n, j] = row
        each(j, NJ, lambda jj: scalar_push(n, SX, s.sx_send.at[n], s.sx_recv.at[n, j], to_j(jj)))

    def scalar_y(n, parts):
        await_bytes(s.sx_recv.at[n, pl.ds(0, NJ - 1)], s.sum_recv.at[n, SX])
        row = jnp.sum(s.sx_recv[n], axis=0)
        full = jnp.where(trait_col == y, row, 0.0)
        for k, part in enumerate(parts):
            full += jnp.where(lane4 == k, part, 0.0)
        s.sy_send[n] = full
        s.sy_recv[n, y] = full
        each(y, ny, lambda yy: scalar_push(n, SY, s.sy_send.at[n], s.sy_recv.at[n, y], to_y(yy)))

    def scalar_end(n):
        await_bytes(s.sy_recv.at[n, pl.ds(0, ny - 1)], s.sum_recv.at[n, SY])
        return jnp.sum(s.sy_recv[n], axis=0)

    def mine(col):
        return jnp.sum(jnp.where(trait_col == y, col, 0.0), axis=0, keepdims=True)

    def gather_wide(it):
        @pl.when(in_jb)
        def _():
            @pl.when(in_zb)
            def _():
                arrived(it, G1, s.g1_recv.at[it, pl.ds(0, ZB - 1)])

            @pl.when(jnp.logical_not(in_zb))
            def _():
                arrived(it, G1, s.g1_recv.at[it])

            s.g2_recv[it, j] = s.g1_recv[it]
            each(j, NJ, lambda jj: start(it, G2, s.g1_recv.at[it], s.g2_recv.at[it, j], to_j(jj)))

    def gather_end(it):
        @pl.when(in_jb)
        def _():
            arrived(it, G2, s.g2_recv.at[it, pl.ds(0, JB - 1)])

        @pl.when(jnp.logical_not(in_jb))
        def _():
            arrived(it, G2, s.g2_recv.at[it])

    def marker_image(it, b):
        cut = cuts[b]
        summed = jnp.concatenate([s.g2_recv[it, b, c] for c in range(ZB)], axis=1)
        q_m = s.mdiag[:, cut] * s.x[:, cut] + s.mscale[:, cut] * summed
        return q_m if it == 0 else q_m + beta * s.q[:, cut]

    rho = alpha = beta = None
    for it in range(ITERS):
        last = it == ITERS - 1
        norm = ITERS + it - 1

        s.a1_send[it] = z_a.astype(BF16)
        s.a1_recv[it, z] = s.a1_send[it]
        each(z, nz, lambda zz: start(it, A1, s.a1_send.at[it], s.a1_recv.at[it, z], to_z(zz)))
        if it == 0:
            for get in gets[2:-1]:
                get.wait()
            plan()
        else:
            scalar_z(norm, [r_a * z_a])
            gather_wide(it - 1)
            scalar_x(norm)
            gather_end(it - 1)

        dot_m, curv_m, rho_m = jnp.zeros((traits, geno), F32), col, col
        for b, cut in enumerate(cuts):
            if it == 0:
                m_inv = 1.0 / s.mdiag[:, cut]
                s.m_inv[:, cut] = m_inv
                r_m = s.mrhs[:, cut]
                x_m = r_m * m_inv
                s.m[:, cut] = x_m
                curv_m += jnp.sum(s.mdiag[:, cut] * x_m * x_m, axis=1, keepdims=True)
            else:
                q_m = marker_image(it - 1, b)
                s.q[:, cut] = q_m
                r_m = mres[:, cut] - alpha * q_m
                x_m = r_m * s.m_inv[:, cut]
            mres[:, cut] = r_m
            s.x[:, cut] = x_m
            rho_m += jnp.sum(r_m * x_m, axis=1, keepdims=True)
            mb = (x_m * s.mscale[:, cut]).astype(BF16)
            dot_m += lax.dot_general(mb, s.g[:, cut], (((1,), (1,)), ((), ())), preferred_element_type=F32)
        own_rows = jnp.sum(jnp.where((blk == gblk) & (lane < geno), z_a, 0.0), axis=0, keepdims=True)
        s.y_send[it] = jnp.where(sub == traits, own_rows, 0.0)
        s.y_send[it, :traits, :geno] = dot_m
        s.y_recv[it, y] = s.y_send[it]
        each(y, ny, lambda yy: start(it, Y, s.y_send.at[it], s.y_recv.at[it, y], to_y(yy)))

        if it == 0:
            serve()

        arrived(it, A1, s.a1_recv.at[it, pl.ds(0, nz - 1)])
        blocks = s.a1_recv[it].astype(F32).reshape(dense, LANES).astype(BF16)
        served = jnp.dot(s.pmat[...], blocks, preferred_element_type=F32)
        s.a2_send[it] = served.reshape(NJ, slots, LANES).astype(BF16)
        s.a2_recv[it, j] = s.a2_send[it, j]
        each(j, NJ, lambda jj: start(it, A2, s.a2_send.at[it, jj], s.a2_recv.at[it, j], to_j(jj)))

        arrived(it, Y, s.y_recv.at[it, pl.ds(0, ny - 1)])
        g = jnp.zeros((traits, LANES), F32)
        for t in range(ny):
            g += s.y_recv[it, t, :traits, :]
            g += jnp.where(trait_col == t, s.y_recv[it, t, traits:traits + 1, :], 0.0)
        gb = g[:, :geno].astype(BF16)
        for b, cut in enumerate(cuts):
            s.r1_send[it, b] = jnp.dot(gb, s.g[:, cut], preferred_element_type=F32)

        def send_r1(jj):
            @pl.when(jj < JB)
            def _():
                start(it, R1, s.r1_send.at[it, jj], s.r1_recv.at[it, j], to_j(jj))

        each(j, NJ, send_r1)
        if it > 0:
            scalar_y(norm, [rho_m])

        if it == 0:
            gets[-1].wait()
        arrived(it, A2, s.a2_recv.at[it, pl.ds(0, NJ - 1)])
        fetched = s.a2_recv[it].reshape(all_slots, LANES)
        s.fetched[...] = jnp.dot(s.placed[...], fetched, preferred_element_type=F32).reshape(LANES // 8, 8, LANES)

        def four(first):
            w = s.w[pl.ds(first, 4)]
            return jnp.concatenate([w[0:2].reshape(2 * LANES, LANES), w[2:4].reshape(2 * LANES, LANES)], axis=1)

        def forward(n, acc):
            rows = s.fetched[n]
            for h in (0, 4):
                a, b, c, d = [jnp.where(sub == s.rows[n * 8 + h + k], rows[h + k:h + k + 1], 0.0) for k in range(4)]
                left = jnp.concatenate([jnp.concatenate([a, c], axis=1), jnp.concatenate([b, d], axis=1)], axis=0)
                acc += lax.dot_general(left.astype(BF16), four(n * 8 + h), (((1,), (1,)), ((), ())),
                                       preferred_element_type=F32)
            return acc

        acc = lax.fori_loop(0, tiles // 8, forward, jnp.zeros((16, 2 * LANES), F32), unroll=2)
        v = acc[:8, :LANES] + acc[8:, LANES:]

        if it > 0:
            rho_next = scalar_end(norm)[:, 0:1]
            beta = rho_next / rho
            rho = rho_next
            beta_y = mine(beta)
            u, v_u, g_u = z_a + beta_y * u, v + beta_y * v_u, g + beta * g_u
        else:
            u, v_u, g_u = z_a, v, g
        g_row = jnp.sum(jnp.where(trait_col == y, g_u, 0.0), axis=0, keepdims=True)
        curv_a = a_diag * u * u + v_u * v_u + jnp.where(sub == 0, g_row * g_row, 0.0)
        scalar_z(it, [curv_a] if it > 0 else [curv_a, r_a * z_a])

        zero = jnp.zeros((8, LANES), F32)
        vb = v.astype(BF16).astype(F32)
        twice = jnp.concatenate([jnp.concatenate([vb, zero], axis=1), jnp.concatenate([zero, vb], axis=1)], axis=0)
        twice = twice.astype(BF16)

        def backward(n, c):
            rows = jnp.zeros((8, LANES), F32)
            for h in (0, 4):
                out = jnp.dot(twice, four(n * 8 + h), preferred_element_type=F32)
                for k in range(4):
                    up, across = k % 2, k // 2
                    part = out[8 * up:8 * up + 8, across * LANES:(across + 1) * LANES]
                    picked = jnp.sum(jnp.where(sub == s.rows[n * 8 + h + k], part, 0.0), axis=0, keepdims=True)
                    rows = jnp.where(sub == h + k, picked, rows)
            s.back[n] = rows
            return c

        lax.fori_loop(0, tiles // 8, backward, 0, unroll=2)
        back = s.back[...].reshape(LANES, LANES).astype(BF16)
        outgoing = jnp.dot(s.placed_t[...], back, preferred_element_type=F32)
        s.b1_send[it] = outgoing.reshape(NJ, slots, LANES).astype(BF16)
        s.b1_recv[it, j] = s.b1_send[it, j]
        each(j, NJ, lambda jj: start(it, B1, s.b1_send.at[it, jj], s.b1_recv.at[it, j], to_j(jj)))

        if it > 0:
            for cut in cuts:
                m = s.m[:, cut]
                msol[:, cut] = alpha * m if it == 1 else msol[:, cut] + alpha * m
                m = s.x[:, cut] + beta * m
                s.m[:, cut] = m
                curv_m += jnp.sum(s.mdiag[:, cut] * m * m, axis=1, keepdims=True)

        @pl.when(in_jb)
        def _():
            s.r1_recv[it, j] = s.r1_send[it, j]
            arrived(it, R1, s.r1_recv.at[it, pl.ds(0, NJ - 1)])
            part = jnp.sum(s.r1_recv[it], axis=0)
            for b in range(ZB):
                s.r2_send[it, b] = part[:, b * LANES:(b + 1) * LANES]

            def send_r2(b, c):
                @pl.when(b * ZS != z)
                def _():
                    start(it, R2, s.r2_send.at[it, b], s.r2_recv.at[it, z], to_z(b * ZS))

                return c

            lax.fori_loop(0, ZB, send_r2, 0)

        scalar_x(it)

        arrived(it, B1, s.b1_recv.at[it, pl.ds(0, NJ - 1)])
        returned = s.b1_recv[it].reshape(all_slots, LANES)
        summed = jnp.dot(s.pmat_t[...], returned, preferred_element_type=F32)
        s.b2_send[it] = summed.reshape(nz, nb, LANES).astype(BF16)
        s.b2_recv[it, z] = s.b2_send[it, z]
        each(z, nz, lambda zz: start(it, B2, s.b2_send.at[it, zz], s.b2_recv.at[it, z], to_z(zz)))

        @pl.when(in_jb & in_zb)
        def _():
            s.r2_recv[it, z] = s.r2_send[it, lax.div(z, ZS)]
            arrived(it, R2, s.r2_recv.at[it, pl.ds(0, nz - 1)])
            part = jnp.sum(s.r2_recv[it], axis=0)
            s.g1_send[it] = part
            s.g1_recv[it, lax.div(z, ZS)] = part
            each(z, nz, lambda zz: start(it, G1, s.g1_send.at[it], s.g1_recv.at[it, lax.div(z, ZS)], to_z(zz)))

        scalar_y(it, [curv_m] if it > 0 else [curv_m, rho_m])

        arrived(it, B2, s.b2_recv.at[it, pl.ds(0, nz - 1)])
        ped = jnp.sum(s.b2_recv[it].astype(F32), axis=0)
        g_row = jnp.sum(jnp.where(trait_col == y, g, 0.0), axis=0, keepdims=True)
        image = a_diag * z_a + ped + jnp.where(blk == gblk, g_row, 0.0)
        q_a = image if it == 0 else image + beta_y * q_a
        sums = scalar_end(it)
        if it == 0:
            rho = sums[:, 1:2]
        alpha = rho / sums[:, 0:1]
        alpha_y = mine(alpha)
        sol_a = sol_a + alpha_y * u
        r_a = r_a - alpha_y * q_a
        z_a = r_a * a_inv

    s.f_send[0] = sol_a
    s.f_send[1] = r_a
    s.f_recv[y] = s.f_send[...]
    each(y, ny, lambda yy: push(s.f_send, s.f_recv.at[y], s.once_send.at[1], s.once_recv.at[1], to_y(yy)))
    gather_wide(it)
    for cut in cuts:
        msol[:, cut] = msol[:, cut] + alpha * s.m[:, cut]
    gather_end(it)
    for b, cut in enumerate(cuts):
        mres[:, cut] = mres[:, cut] - alpha * marker_image(it, b)
    await_bytes(s.f_recv.at[pl.ds(0, ny - 1)], s.once_recv.at[1])
    for t in range(traits):
        for k in range(nb):
            asol[t:t + 1, k * LANES:(k + 1) * LANES] = s.f_recv[t, 0, k:k + 1, :]
            ares[t:t + 1, k * LANES:(k + 1) * LANES] = s.f_recv[t, 1, k:k + 1, :]

    await_bytes(s.id_recv.at[pl.ds(0, NJ - 1)], s.once_send.at[0])
    await_bytes(s.f_recv.at[pl.ds(0, ny - 1)], s.once_send.at[1])
    for n in range(SUMS):
        for step, ref, count in ((SZ, s.sz_recv, nz - 1), (SX, s.sx_recv, NJ - 1), (SY, s.sy_recv, ny - 1)):
            await_bytes(ref.at[n, pl.ds(0, count)], s.sum_send.at[n, step])
    for it in range(ITERS):
        def gone(stage, ref, count, it=it):
            await_bytes(ref.at[it, pl.ds(0, count)], s.send.at[it, stage])

        for stage, ref, count in ((A1, s.a1_recv, nz - 1), (A2, s.a2_recv, NJ - 1), (B1, s.b1_recv, NJ - 1),
                                  (B2, s.b2_recv, nz - 1), (Y, s.y_recv, ny - 1)):
            gone(stage, ref, count)

        @pl.when(in_jb)
        def _():
            gone(R1, s.r1_recv, JB - 1)
            gone(G2, s.g2_recv, NJ - 1)

            @pl.when(in_zb)
            def _():
                gone(R2, s.r2_recv, ZB - 1)
                gone(G1, s.r2_recv, nz - 1)

            @pl.when(jnp.logical_not(in_zb))
            def _():
                gone(R2, s.r2_recv, ZB)

        @pl.when(jnp.logical_not(in_jb))
        def _():
            gone(R1, s.r1_recv, JB)


def body(animal_rhs, marker_rhs, animal_diagonal, marker_diagonal, marker_scale, genotypes, tile_weights,
         tile_rows, tile_owner, tile_local, tile_count, genotyped_block):
    traits, animals = animal_rhs.shape
    markers = marker_rhs.shape[1]
    tiles = tile_weights.shape[0]
    nz, ny = lax.axis_size(ANIMALS) // NJ, lax.axis_size(SNPS)
    nb, slots = animals // LANES, nz * CAP
    every = NJ * slots
    wide = ZB * LANES

    def f32(*shape):
        return pltpu.VMEM(shape, F32)

    def b16(*shape):
        return pltpu.VMEM(shape, BF16)

    dma = pltpu.SemaphoreType.DMA
    scratch = dict(
        arhs=f32(traits, animals), adiag=f32(nb, LANES), mrhs=f32(traits, markers), mdiag=f32(1, markers),
        mscale=f32(1, markers), owner=pltpu.VMEM((1, tiles), I32), local=pltpu.VMEM((1, tiles), I32),
        rows=pltpu.SMEM((tiles,), I32),
        w=b16(*tile_weights.shape), g=b16(*genotypes.shape),
        placed=b16(LANES, every), placed_t=b16(every, LANES), table=f32(every, LANES),
        pmat=b16(every, nz * nb), pmat_t=b16(nz * nb, every),
        fetched=f32(LANES // 8, 8, LANES), back=f32(LANES // 8, 8, LANES),
        m=f32(traits, markers), q=f32(traits, markers), x=f32(traits, markers),
        m_inv=f32(1, markers),
        id_send=b16(NJ, slots, LANES), id_recv=b16(NJ, slots, LANES),
        a1_send=b16(ITERS, nb, LANES), a1_recv=b16(ITERS, nz, nb, LANES),
        a2_send=b16(ITERS, NJ, slots, LANES), a2_recv=b16(ITERS, NJ, slots, LANES),
        b1_send=b16(ITERS, NJ, slots, LANES), b1_recv=b16(ITERS, NJ, slots, LANES),
        b2_send=b16(ITERS, nz, nb, LANES), b2_recv=b16(ITERS, nz, nb, LANES),
        y_send=f32(ITERS, 8, LANES), y_recv=f32(ITERS, ny, 8, LANES),
        r1_send=f32(ITERS, JB, traits, wide), r1_recv=f32(ITERS, NJ, traits, wide),
        r2_send=f32(ITERS, ZB, traits, LANES), r2_recv=f32(ITERS, nz, traits, LANES),
        g1_send=f32(ITERS, traits, LANES), g1_recv=f32(ITERS, ZB, traits, LANES),
        g2_recv=f32(ITERS, JB, ZB, traits, LANES),
        sz_send=f32(SUMS, 1, LANES), sz_recv=f32(SUMS, nz, 1, LANES),
        sx_send=f32(SUMS, 1, LANES), sx_recv=f32(SUMS, NJ, 1, LANES),
        sy_send=f32(SUMS, traits, LANES), sy_recv=f32(SUMS, ny, traits, LANES),
        f_send=f32(2, nb, LANES), f_recv=f32(ny, 2, nb, LANES),
        get=dma((10,)), once_send=dma((2,)), once_recv=dma((2,)),
        send=dma((ITERS, STAGES)), recv=dma((ITERS, STAGES)),
        sum_send=dma((SUMS, STEPS)), sum_recv=dma((SUMS, STEPS)),
    )

    def run(*refs):
        first = len(refs) - len(scratch)
        kernel(nz, ny, *refs[:first], SimpleNamespace(**dict(zip(scratch, refs[first:]))))

    outs = pl.pallas_call(
        run,
        out_shape=[jax.ShapeDtypeStruct(a.shape, F32) for a in (animal_rhs, marker_rhs, animal_rhs, marker_rhs)],
        in_specs=[pl.BlockSpec(memory_space=pl.ANY)] * 10 + [pl.BlockSpec(memory_space=pltpu.SMEM)] * 2,
        out_specs=[pl.BlockSpec(memory_space=pltpu.VMEM)] * 4,
        scratch_shapes=list(scratch.values()),
        compiler_params=pltpu.CompilerParams(collective_id=0, has_side_effects=True, vmem_limit_bytes=60 * 2**20),
    )(animal_rhs, marker_rhs, animal_diagonal.reshape(nb, LANES), marker_diagonal,
      marker_scale, genotypes, tile_weights, tile_rows, tile_owner.reshape(1, tiles),
      tile_local.reshape(1, tiles), tile_count, genotyped_block)

    def leave(*refs):
        copies = [pltpu.make_async_copy(refs[k], refs[4 + k], refs[8].at[k]) for k in range(4)]
        for copy in copies:
            copy.start()
        for copy in copies:
            copy.wait()

    return pl.pallas_call(
        leave,
        out_shape=[jax.ShapeDtypeStruct(a.shape, F32) for a in outs],
        in_specs=[pl.BlockSpec(memory_space=pl.ANY)] * 4,
        out_specs=[pl.BlockSpec(memory_space=pl.ANY)] * 4,
        scratch_shapes=[dma((4,))],
        compiler_params=pltpu.CompilerParams(vmem_limit_bytes=60 * 2**20),
    )(*outs)


def solution(mesh):
    placed = (P(None, ANIMALS), P(None, SNPS), P(ANIMALS), P(SNPS), P(SNPS), P(ANIMALS, SNPS),
              P(ANIMALS, None, None), P(ANIMALS), P(ANIMALS, None), P(ANIMALS), P(ANIMALS), P(ANIMALS))
    return jax.shard_map(
        body, mesh=mesh, in_specs=placed,
        out_specs=(P(None, ANIMALS), P(None, SNPS), P(None, ANIMALS), P(None, SNPS)), check_vma=False)
```

time: 1680 us -> 121 us (0.07)
  waiting for transfers between devices: 1010 us -> 0 us
  blocking collectives: 527 us -> 0 us
  Pallas kernels: 0 us -> 119 us
  starting transfers between devices: 70.9 us -> 0 us
  matrix products: 30.5 us -> 0 us
    psum x3 -> x0, waiting for transfers between devices: 947 us -> none  [body(): marker_back = lax.psum(marker_part, 'animals')]
    psum x8 -> x0, blocking collectives: 527 us -> none  [the longest x3 300 us: norm_sum(): lax.psum(local_inner(first_u, first_m, second_u, second_m), ('animals', '...]
    pallas_call x0 -> x2, Pallas kernels: none -> 119 us  [the longest x1 111 us: body(): pl.pallas_call(run, out_shape=[jax.ShapeDtypeStruct(a.shape, F32) for a i...]
    all_to_all x7 -> x0, starting transfers between devices: 70.8 us -> none  [the longest x3 25.4 us: body(): lax.all_to_all(served.reshape(group_size, capacity, traits * block_size),...]
    all_to_all x7 -> x0, waiting for transfers between devices: 64.2 us -> none  [the longest x3 50.1 us: body(): lax.all_to_all(served.reshape(group_size, capacity, traits * block_size),...]
    dot_general x30 -> x0, matrix products: 30.5 us -> none  [the longest x3 12 us: body(): jnp.einsum('tik,tsk->tsi', tile_weights, fetched, preferred_element_type=...]
  transfers between devices with their start and end apart: 10 -> 0, of which waited for: 7 -> 0; matrix products, arithmetic and copies ran while one was open for 1% -> 0% of each run, Pallas kernels for 0% -> 0%
where the time goes in v1:
time: 121 us
  Pallas kernels  119 us (98%)
  between operations  1.93 us (2%)
    pallas_call x1, Pallas kernels, body(): pl.pallas_call(run, out_shape=[jax.ShapeDtypeStruct(a.shape, F32) for a i...  111 us
    pallas_call x1, Pallas kernels, body(): pl.pallas_call(leave, out_shape=[jax.ShapeDtypeStruct(a.shape, F32) for a...  8.21 us

profile of v1, /device:TPU:1, one launch (start us, length us, event | category | flops | bytes accessed | tf_op | source)
XLA Modules:
  0.0 121.1 jit_solution(401828513890796567)
XLA Ops:
  1.9 110.9 %shard_map.147 = (f32[4,1024]{1,0:T(4,128)}, f32[4,6272]{1,0:T(4,128)}, f32[4,1024]{1,0:T(4,128)}, f32[4,6272]{1,0:T(4,128)}) custom-call(f32[4,1024]{1,0:T(4,128)} %refs_0_.1, f32[4,6272]{1,0:T(4,128)} %refs_1_.1, f32[8,128]{1,0:T(8,128)} %bitcast.3, f32[6272]{0:T(1024)} %refs_3_.1, f32[6272]{0:T(1024)} %refs_4_.1, bf16[64,6272]{1,0:T(8,128)(2,1)} %refs_5_.1, ...), custom_call_target="tpu_custom_call" | custom-call | tf_op jit(solution)/shard_map/pallas_call | solution.py:494
  112.9 8.2 %shard_map.148 = (f32[4,1024]{1,0:T(4,128)}, f32[4,6272]{1,0:T(4,128)}, f32[4,1024]{1,0:T(4,128)}, f32[4,6272]{1,0:T(4,128)}) custom-call(f32[4,1024]{1,0:T(4,128)} %get-tuple-element.8.refs_0_, f32[4,6272]{1,0:T(4,128)} %get-tuple-element.9.refs_1_, f32[4,1024]{1,0:T(4,128)} %get-tuple-element.10.refs_2_, f32[4,6272]{1,0:T(4,128)} %get-tuple-element.11.refs_3_), custom_call_target="tpu_custom_call" | custom-call | tf_op jit(solution)/shard_map/pallas_call | solution.py:512

commit v2 on v1

--- a/solution.py
+++ b/solution.py
@@ -217,9 +217,19 @@
             for get in gets[2:-1]:
                 get.wait()
             plan()
+            serve()
         else:
             scalar_z(norm, [r_a * z_a])
             gather_wide(it - 1)
+
+        arrived(it, A1, s.a1_recv.at[it, pl.ds(0, nz - 1)])
+        blocks = s.a1_recv[it].astype(F32).reshape(dense, LANES).astype(BF16)
+        served = jnp.dot(s.pmat[...], blocks, preferred_element_type=F32)
+        s.a2_send[it] = served.reshape(NJ, slots, LANES).astype(BF16)
+        s.a2_recv[it, j] = s.a2_send[it, j]
+        each(j, NJ, lambda jj: start(it, A2, s.a2_send.at[it, jj], s.a2_recv.at[it, j], to_j(jj)))
+
+        if it > 0:
             scalar_x(norm)
             gather_end(it - 1)
 
@@ -248,15 +258,30 @@
         s.y_recv[it, y] = s.y_send[it]
         each(y, ny, lambda yy: start(it, Y, s.y_send.at[it], s.y_recv.at[it, y], to_y(yy)))
 
+        if it > 0:
+            scalar_y(norm, [rho_m])
+
         if it == 0:
-            serve()
-
-        arrived(it, A1, s.a1_recv.at[it, pl.ds(0, nz - 1)])
-        blocks = s.a1_recv[it].astype(F32).reshape(dense, LANES).astype(BF16)
-        served = jnp.dot(s.pmat[...], blocks, preferred_element_type=F32)
-        s.a2_send[it] = served.reshape(NJ, slots, LANES).astype(BF16)
-        s.a2_recv[it, j] = s.a2_send[it, j]
-        each(j, NJ, lambda jj: start(it, A2, s.a2_send.at[it, jj], s.a2_recv.at[it, j], to_j(jj)))
+            gets[-1].wait()
+        arrived(it, A2, s.a2_recv.at[it, pl.ds(0, NJ - 1)])
+        fetched = s.a2_recv[it].reshape(all_slots, LANES)
+        s.fetched[...] = jnp.dot(s.placed[...], fetched, preferred_element_type=F32).reshape(LANES // 8, 8, LANES)
+
+        def four(first):
+            w = s.w[pl.ds(first, 4)]
+            return jnp.concatenate([w[0:2].reshape(2 * LANES, LANES), w[2:4].reshape(2 * LANES, LANES)], axis=1)
+
+        def forward(n, acc):
+            rows = s.fetched[n]
+            for h in (0, 4):
+                a, b, c, d = [jnp.where(sub == s.rows[n * 8 + h + k], rows[h + k:h + k + 1], 0.0) for k in range(4)]
+                left = jnp.concatenate([jnp.concatenate([a, c], axis=1), jnp.concatenate([b, d], axis=1)], axis=0)
+                acc += lax.dot_general(left.astype(BF16), four(n * 8 + h), (((1,), (1,)), ((), ())),
+                                       preferred_element_type=F32)
+            return acc
+
+        acc = lax.fori_loop(0, tiles // 8, forward, jnp.zeros((16, 2 * LANES), F32), unroll=7)
+        v = acc[:8, :LANES] + acc[8:, LANES:]
 
         arrived(it, Y, s.y_recv.at[it, pl.ds(0, ny - 1)])
         g = jnp.zeros((traits, LANES), F32)
@@ -273,31 +298,6 @@
                 start(it, R1, s.r1_send.at[it, jj], s.r1_recv.at[it, j], to_j(jj))
 
         each(j, NJ, send_r1)
-        if it > 0:
-            scalar_y(norm, [rho_m])
-
-        if it == 0:
-            gets[-1].wait()
-        arrived(it, A2, s.a2_recv.at[it, pl.ds(0, NJ - 1)])
-        fetched = s.a2_recv[it].reshape(all_slots, LANES)
-        s.fetched[...] = jnp.dot(s.placed[...], fetched, preferred_element_type=F32).reshape(LANES // 8, 8, LANES)
-
-        def four(first):
-            w = s.w[pl.ds(first, 4)]
-            return jnp.concatenate([w[0:2].reshape(2 * LANES, LANES), w[2:4].reshape(2 * LANES, LANES)], axis=1)
-
-        def forward(n, acc):
-            rows = s.fetched[n]
-            for h in (0, 4):
-                a, b, c, d = [jnp.where(sub == s.rows[n * 8 + h + k], rows[h + k:h + k + 1], 0.0) for k in range(4)]
-                left = jnp.concatenate([jnp.concatenate([a, c], axis=1), jnp.concatenate([b, d], axis=1)], axis=0)
-                acc += lax.dot_general(left.astype(BF16), four(n * 8 + h), (((1,), (1,)), ((), ())),
-                                       preferred_element_type=F32)
-            return acc
-
-        acc = lax.fori_loop(0, tiles // 8, forward, jnp.zeros((16, 2 * LANES), F32), unroll=2)
-        v = acc[:8, :LANES] + acc[8:, LANES:]
-
         if it > 0:
             rho_next = scalar_end(norm)[:, 0:1]
             beta = rho_next / rho
@@ -327,7 +327,7 @@
             s.back[n] = rows
             return c
 
-        lax.fori_loop(0, tiles // 8, backward, 0, unroll=2)
+        lax.fori_loop(0, tiles // 8, backward, 0, unroll=7)
         back = s.back[...].reshape(LANES, LANES).astype(BF16)
         outgoing = jnp.dot(s.placed_t[...], back, preferred_element_type=F32)
         s.b1_send[it] = outgoing.reshape(NJ, slots, LANES).astype(BF16)
@@ -503,18 +503,23 @@
       tile_local.reshape(1, tiles), tile_count, genotyped_block)
 
     def leave(*refs):
-        copies = [pltpu.make_async_copy(refs[k], refs[4 + k], refs[8].at[k]) for k in range(4)]
-        for copy in copies:
-            copy.start()
-        for copy in copies:
-            copy.wait()
+        sources, results, stages, sems = refs[:4], refs[4:8], refs[8:12], refs[12]
+        reads = [pltpu.make_async_copy(a, b, sems.at[k]) for k, (a, b) in enumerate(zip(sources, stages))]
+        writes = [pltpu.make_async_copy(a, b, sems.at[4 + k]) for k, (a, b) in enumerate(zip(stages, results))]
+        for read in reads:
+            read.start()
+        for read, write in zip(reads, writes):
+            read.wait()
+            write.start()
+        for write in writes:
+            write.wait()
 
     return pl.pallas_call(
         leave,
         out_shape=[jax.ShapeDtypeStruct(a.shape, F32) for a in outs],
         in_specs=[pl.BlockSpec(memory_space=pl.ANY)] * 4,
         out_specs=[pl.BlockSpec(memory_space=pl.ANY)] * 4,
-        scratch_shapes=[dma((4,))],
+        scratch_shapes=[pltpu.VMEM(a.shape, F32) for a in outs] + [dma((8,))],
         compiler_params=pltpu.CompilerParams(vmem_limit_bytes=60 * 2**20),
     )(*outs)
 

time: 121 us -> 112 us (0.926)
  Pallas kernels: 119 us -> 109 us
    pallas_call x1, Pallas kernels: 8.21 us -> 1.69 us  [body(): pl.pallas_call(leave, out_shape=[jax.ShapeDtypeStruct(a.shape, F32) for a...]
    pallas_call x1, Pallas kernels: 111 us -> 108 us  [body(): pl.pallas_call(run, out_shape=[jax.ShapeDtypeStruct(a.shape, F32) for a i...]
where the time goes in v2:
time: 112 us; the launch traced here: 111 us
  Pallas kernels  109 us (97%)
  between operations  1.93 us (2%)
    pallas_call x1, Pallas kernels, body(): pl.pallas_call(run, out_shape=[jax.ShapeDtypeStruct(a.shape, F32) for a i...  108 us

profile of v2, /device:TPU:1, one launch (start us, length us, event | category | flops | bytes accessed | tf_op | source)
XLA Modules:
  0.0 111.3 jit_solution(2898268423299913015)
XLA Ops:
  1.9 107.7 %shard_map.147 = (f32[4,1024]{1,0:T(4,128)}, f32[4,6272]{1,0:T(4,128)}, f32[4,1024]{1,0:T(4,128)}, f32[4,6272]{1,0:T(4,128)}) custom-call(f32[4,1024]{1,0:T(4,128)} %refs_0_.1, f32[4,6272]{1,0:T(4,128)} %refs_1_.1, f32[8,128]{1,0:T(8,128)} %bitcast.3, f32[6272]{0:T(1024)} %refs_3_.1, f32[6272]{0:T(1024)} %refs_4_.1, bf16[64,6272]{1,0:T(8,128)(2,1)} %refs_5_.1, ...), custom_call_target="tpu_custom_call" | custom-call | tf_op jit(solution)/shard_map/pallas_call | solution.py:494
  109.6 1.7 %shard_map.148 = (f32[4,1024]{1,0:T(4,128)}, f32[4,6272]{1,0:T(4,128)}, f32[4,1024]{1,0:T(4,128)}, f32[4,6272]{1,0:T(4,128)}) custom-call(f32[4,1024]{1,0:T(4,128)} %get-tuple-element.8.refs_0_, f32[4,6272]{1,0:T(4,128)} %get-tuple-element.9.refs_1_, f32[4,1024]{1,0:T(4,128)} %get-tuple-element.10.refs_2_, f32[4,6272]{1,0:T(4,128)} %get-tuple-element.11.refs_3_), custom_call_target="tpu_custom_call" | custom-call | tf_op jit(solution)/shard_map/pallas_call | solution.py:517

commit v3 on v2

--- a/solution.py
+++ b/solution.py
@@ -14,7 +14,7 @@
 LANES = 128
 A1, A2, B1, B2, Y, R1, R2, G1, G2, STAGES = range(10)
 SZ, SX, SY, STEPS = range(4)
-SUMS = 2 * ITERS - 1
+SUMS = 2 * ITERS
 ANIMALS, SNPS = "animals", "snps"
 MESH = pl.DeviceIdType.MESH
 F32, BF16, I32 = jnp.float32, jnp.bfloat16, jnp.int32
@@ -51,16 +51,16 @@
     def to_y(yy):
         return {ANIMALS: me, SNPS: yy}
 
-    def each(here, count, act):
+    def others(here, count):
         half = count // 2
-        act(lax.rem(here + half, count))
-
-        def step(d, c):
-            act(lax.rem(here + half - d, count))
-            act(lax.rem(here + half + d, count))
-            return c
-
-        lax.fori_loop(1, half, step, 0)
+        order = [half] + [half + d for k in range(1, half) for d in (-k, k)]
+        return [lax.rem(here + d, count) for d in order]
+
+    peers_z, peers_j, peers_y = others(z, nz), others(j, NJ), others(y, ny)
+
+    def each(peers, act):
+        for peer in peers:
+            act(peer)
 
     def push(src, dst, send, recv, device):
         pltpu.make_async_remote_copy(src_ref=src, dst_ref=dst, send_sem=send, recv_sem=recv,
@@ -74,9 +74,9 @@
     def greet(device):
         pl.semaphore_signal(barrier, inc=1, device_id=device, device_id_type=MESH)
 
-    each(z, nz, lambda zz: greet(to_z(zz)))
-    each(j, NJ, lambda jj: greet(to_j(jj)))
-    each(y, ny, lambda yy: greet(to_y(yy)))
+    each(peers_z, lambda zz: greet(to_z(zz)))
+    each(peers_j, lambda jj: greet(to_j(jj)))
+    each(peers_y, lambda yy: greet(to_y(yy)))
 
     pairs = ((arhs_h, s.arhs), (adiag_h, s.adiag), (mrhs_h, s.mrhs), (mdiag_h, s.mdiag.at[0]), (mscale_h, s.mscale.at[0]),
              (owner_h, s.owner), (local_h, s.local), (rows_h, s.rows), (geno_h, s.g), (w_h, s.w))
@@ -97,8 +97,6 @@
     for k in range(nb):
         row = jnp.where(trait_col == y, s.arhs[:, k * LANES:(k + 1) * LANES], 0.0)
         r_a = jnp.where(blk == k, jnp.sum(row, axis=0, keepdims=True), r_a)
-    z_a = r_a * a_inv
-    sol_a = jnp.zeros((nb, LANES), F32)
     gblk = gblk_s[0]
     cuts = [slice(b * wide, (b + 1) * wide) for b in range(JB)]
     col = jnp.zeros((traits, 1), F32)
@@ -115,7 +113,7 @@
         asked = jnp.sum(hit * (s.local[...] + 1).astype(F32), axis=1, keepdims=True)
         asked = jnp.broadcast_to(asked, (all_slots, LANES))
         s.id_send[...] = asked.reshape(NJ, slots, LANES).astype(BF16)
-        each(j, NJ, lambda jj: push(s.id_send.at[jj], s.id_recv.at[j], s.once_send.at[0], s.once_recv.at[0], to_j(jj)))
+        each(peers_j, lambda jj: push(s.id_send.at[jj], s.id_recv.at[j], s.once_send.at[0], s.once_recv.at[0], to_j(jj)))
         s.id_recv[j] = s.id_send[j]
         s.table[...] = jnp.zeros_like(s.table)
         s.table[:, :tiles] = hit
@@ -133,6 +131,14 @@
         s.pmat[...] = pmat.astype(BF16)
         s.pmat_t[...] = pmat.T.astype(BF16)
 
+    def begin():
+        for cut in cuts:
+            s.m_inv[:, cut] = 1.0 / s.mdiag[:, cut]
+            mres[:, cut] = s.mrhs[:, cut]
+            for ref in (s.x, s.q, s.m, msol):
+                ref[:, cut] = jnp.zeros((traits, wide), F32)
+        s.g2_recv[0] = jnp.zeros(s.g2_recv.shape[1:], F32)
+
     pl.semaphore_wait(barrier, nz + NJ + ny - 3)
 
     def start(it, stage, src, dst, device):
@@ -150,14 +156,14 @@
             row = jnp.where(lane4[:1] == k, total(part), row)
         s.sz_send[n] = row
         s.sz_recv[n, z] = row
-        each(z, nz, lambda zz: scalar_push(n, SZ, s.sz_send.at[n], s.sz_recv.at[n, z], to_z(zz)))
+        each(peers_z, lambda zz: scalar_push(n, SZ, s.sz_send.at[n], s.sz_recv.at[n, z], to_z(zz)))
 
     def scalar_x(n):
         await_bytes(s.sz_recv.at[n, pl.ds(0, nz - 1)], s.sum_recv.at[n, SZ])
         row = jnp.sum(s.sz_recv[n], axis=0)
         s.sx_send[n] = row
         s.sx_recv[n, j] = row
-        each(j, NJ, lambda jj: scalar_push(n, SX, s.sx_send.at[n], s.sx_recv.at[n, j], to_j(jj)))
+        each(peers_j, lambda jj: scalar_push(n, SX, s.sx_send.at[n], s.sx_recv.at[n, j], to_j(jj)))
 
     def scalar_y(n, parts):
         await_bytes(s.sx_recv.at[n, pl.ds(0, NJ - 1)], s.sum_recv.at[n, SX])
@@ -167,7 +173,7 @@
             full += jnp.where(lane4 == k, part, 0.0)
         s.sy_send[n] = full
         s.sy_recv[n, y] = full
-        each(y, ny, lambda yy: scalar_push(n, SY, s.sy_send.at[n], s.sy_recv.at[n, y], to_y(yy)))
+        each(peers_y, lambda yy: scalar_push(n, SY, s.sy_send.at[n], s.sy_recv.at[n, y], to_y(yy)))
 
     def scalar_end(n):
         await_bytes(s.sy_recv.at[n, pl.ds(0, ny - 1)], s.sum_recv.at[n, SY])
@@ -187,39 +193,42 @@
             def _():
                 arrived(it, G1, s.g1_recv.at[it])
 
-            s.g2_recv[it, j] = s.g1_recv[it]
-            each(j, NJ, lambda jj: start(it, G2, s.g1_recv.at[it], s.g2_recv.at[it, j], to_j(jj)))
+            s.g2_recv[it + 1, j] = s.g1_recv[it]
+            each(peers_j, lambda jj: start(it, G2, s.g1_recv.at[it], s.g2_recv.at[it + 1, j], to_j(jj)))
 
     def gather_end(it):
         @pl.when(in_jb)
         def _():
-            arrived(it, G2, s.g2_recv.at[it, pl.ds(0, JB - 1)])
+            arrived(it, G2, s.g2_recv.at[it + 1, pl.ds(0, JB - 1)])
 
         @pl.when(jnp.logical_not(in_jb))
         def _():
-            arrived(it, G2, s.g2_recv.at[it])
-
-    def marker_image(it, b):
+            arrived(it, G2, s.g2_recv.at[it + 1])
+
+    def marker_image(n, b, beta):
         cut = cuts[b]
-        summed = jnp.concatenate([s.g2_recv[it, b, c] for c in range(ZB)], axis=1)
-        q_m = s.mdiag[:, cut] * s.x[:, cut] + s.mscale[:, cut] * summed
-        return q_m if it == 0 else q_m + beta * s.q[:, cut]
-
-    rho = alpha = beta = None
-    for it in range(ITERS):
-        last = it == ITERS - 1
-        norm = ITERS + it - 1
+        summed = jnp.concatenate([s.g2_recv[n, b, c] for c in range(ZB)], axis=1)
+        return s.mdiag[:, cut] * s.x[:, cut] + s.mscale[:, cut] * summed + beta * s.q[:, cut]
+
+    def iterate(it, held):
+        z_a, r_a, q_a, u, sol_a, v_u, g_u, alpha, beta, rho = held
+        norm = ITERS + it
 
         s.a1_send[it] = z_a.astype(BF16)
         s.a1_recv[it, z] = s.a1_send[it]
-        each(z, nz, lambda zz: start(it, A1, s.a1_send.at[it], s.a1_recv.at[it, z], to_z(zz)))
-        if it == 0:
+        each(peers_z, lambda zz: start(it, A1, s.a1_send.at[it], s.a1_recv.at[it, z], to_z(zz)))
+        scalar_z(norm, [r_a * z_a])
+
+        @pl.when(it == 0)
+        def _():
             for get in gets[2:-1]:
                 get.wait()
             plan()
+            begin()
             serve()
-        else:
-            scalar_z(norm, [r_a * z_a])
+
+        @pl.when(it > 0)
+        def _():
             gather_wide(it - 1)
 
         arrived(it, A1, s.a1_recv.at[it, pl.ds(0, nz - 1)])
@@ -227,26 +236,20 @@
         served = jnp.dot(s.pmat[...], blocks, preferred_element_type=F32)
         s.a2_send[it] = served.reshape(NJ, slots, LANES).astype(BF16)
         s.a2_recv[it, j] = s.a2_send[it, j]
-        each(j, NJ, lambda jj: start(it, A2, s.a2_send.at[it, jj], s.a2_recv.at[it, j], to_j(jj)))
-
-        if it > 0:
-            scalar_x(norm)
+        each(peers_j, lambda jj: start(it, A2, s.a2_send.at[it, jj], s.a2_recv.at[it, j], to_j(jj)))
+
+        scalar_x(norm)
+
+        @pl.when(it > 0)
+        def _():
             gather_end(it - 1)
 
         dot_m, curv_m, rho_m = jnp.zeros((traits, geno), F32), col, col
         for b, cut in enumerate(cuts):
-            if it == 0:
-                m_inv = 1.0 / s.mdiag[:, cut]
-                s.m_inv[:, cut] = m_inv
-                r_m = s.mrhs[:, cut]
-                x_m = r_m * m_inv
-                s.m[:, cut] = x_m
-                curv_m += jnp.sum(s.mdiag[:, cut] * x_m * x_m, axis=1, keepdims=True)
-            else:
-                q_m = marker_image(it - 1, b)
-                s.q[:, cut] = q_m
-                r_m = mres[:, cut] - alpha * q_m
-                x_m = r_m * s.m_inv[:, cut]
+            q_m = marker_image(it, b, beta)
+            r_m = mres[:, cut] - alpha * q_m
+            x_m = r_m * s.m_inv[:, cut]
+            s.q[:, cut] = q_m
             mres[:, cut] = r_m
             s.x[:, cut] = x_m
             rho_m += jnp.sum(r_m * x_m, axis=1, keepdims=True)
@@ -256,13 +259,14 @@
         s.y_send[it] = jnp.where(sub == traits, own_rows, 0.0)
         s.y_send[it, :traits, :geno] = dot_m
         s.y_recv[it, y] = s.y_send[it]
-        each(y, ny, lambda yy: start(it, Y, s.y_send.at[it], s.y_recv.at[it, y], to_y(yy)))
-
-        if it > 0:
-            scalar_y(norm, [rho_m])
-
-        if it == 0:
+        each(peers_y, lambda yy: start(it, Y, s.y_send.at[it], s.y_recv.at[it, y], to_y(yy)))
+
+        scalar_y(norm, [rho_m])
+
+        @pl.when(it == 0)
+        def _():
             gets[-1].wait()
+
         arrived(it, A2, s.a2_recv.at[it, pl.ds(0, NJ - 1)])
         fetched = s.a2_recv[it].reshape(all_slots, LANES)
         s.fetched[...] = jnp.dot(s.placed[...], fetched, preferred_element_type=F32).reshape(LANES // 8, 8, LANES)
@@ -280,7 +284,7 @@
                                        preferred_element_type=F32)
             return acc
 
-        acc = lax.fori_loop(0, tiles // 8, forward, jnp.zeros((16, 2 * LANES), F32), unroll=7)
+        acc = lax.fori_loop(0, tiles // 8, forward, jnp.zeros((16, 2 * LANES), F32), unroll=True)
         v = acc[:8, :LANES] + acc[8:, LANES:]
 
         arrived(it, Y, s.y_recv.at[it, pl.ds(0, ny - 1)])
@@ -297,18 +301,13 @@
             def _():
                 start(it, R1, s.r1_send.at[it, jj], s.r1_recv.at[it, j], to_j(jj))
 
-        each(j, NJ, send_r1)
-        if it > 0:
-            rho_next = scalar_end(norm)[:, 0:1]
-            beta = rho_next / rho
-            rho = rho_next
-            beta_y = mine(beta)
-            u, v_u, g_u = z_a + beta_y * u, v + beta_y * v_u, g + beta * g_u
-        else:
-            u, v_u, g_u = z_a, v, g
+        each(peers_j, send_r1)
+        rho_next = scalar_end(norm)[:, 0:1]
+        beta = jnp.where(it == 0, 0.0, rho_next / rho)
+        beta_y = mine(beta)
+        u, v_u, g_u = z_a + beta_y * u, v + beta_y * v_u, g + beta * g_u
         g_row = jnp.sum(jnp.where(trait_col == y, g_u, 0.0), axis=0, keepdims=True)
-        curv_a = a_diag * u * u + v_u * v_u + jnp.where(sub == 0, g_row * g_row, 0.0)
-        scalar_z(it, [curv_a] if it > 0 else [curv_a, r_a * z_a])
+        scalar_z(it, [a_diag * u * u + v_u * v_u + jnp.where(sub == 0, g_row * g_row, 0.0)])
 
         zero = jnp.zeros((8, LANES), F32)
         vb = v.astype(BF16).astype(F32)
@@ -327,20 +326,19 @@
             s.back[n] = rows
             return c
 
-        lax.fori_loop(0, tiles // 8, backward, 0, unroll=7)
+        lax.fori_loop(0, tiles // 8, backward, 0, unroll=True)
         back = s.back[...].reshape(LANES, LANES).astype(BF16)
         outgoing = jnp.dot(s.placed_t[...], back, preferred_element_type=F32)
         s.b1_send[it] = outgoing.reshape(NJ, slots, LANES).astype(BF16)
         s.b1_recv[it, j] = s.b1_send[it, j]
-        each(j, NJ, lambda jj: start(it, B1, s.b1_send.at[it, jj], s.b1_recv.at[it, j], to_j(jj)))
-
-        if it > 0:
-            for cut in cuts:
-                m = s.m[:, cut]
-                msol[:, cut] = alpha * m if it == 1 else msol[:, cut] + alpha * m
-                m = s.x[:, cut] + beta * m
-                s.m[:, cut] = m
-                curv_m += jnp.sum(s.mdiag[:, cut] * m * m, axis=1, keepdims=True)
+        each(peers_j, lambda jj: start(it, B1, s.b1_send.at[it, jj], s.b1_recv.at[it, j], to_j(jj)))
+
+        for cut in cuts:
+            m = s.m[:, cut]
+            msol[:, cut] = msol[:, cut] + alpha * m
+            m = s.x[:, cut] + beta * m
+            s.m[:, cut] = m
+            curv_m += jnp.sum(s.mdiag[:, cut] * m * m, axis=1, keepdims=True)
 
         @pl.when(in_jb)
         def _():
@@ -350,14 +348,10 @@
             for b in range(ZB):
                 s.r2_send[it, b] = part[:, b * LANES:(b + 1) * LANES]
 
-            def send_r2(b, c):
+            for b in range(ZB):
                 @pl.when(b * ZS != z)
-                def _():
+                def _(b=b):
                     start(it, R2, s.r2_send.at[it, b], s.r2_recv.at[it, z], to_z(b * ZS))
-
-                return c
-
-            lax.fori_loop(0, ZB, send_r2, 0)
 
         scalar_x(it)
 
@@ -366,7 +360,7 @@
         summed = jnp.dot(s.pmat_t[...], returned, preferred_element_type=F32)
         s.b2_send[it] = summed.reshape(nz, nb, LANES).astype(BF16)
         s.b2_recv[it, z] = s.b2_send[it, z]
-        each(z, nz, lambda zz: start(it, B2, s.b2_send.at[it, zz], s.b2_recv.at[it, z], to_z(zz)))
+        each(peers_z, lambda zz: start(it, B2, s.b2_send.at[it, zz], s.b2_recv.at[it, z], to_z(zz)))
 
         @pl.when(in_jb & in_zb)
         def _():
@@ -375,34 +369,36 @@
             part = jnp.sum(s.r2_recv[it], axis=0)
             s.g1_send[it] = part
             s.g1_recv[it, lax.div(z, ZS)] = part
-            each(z, nz, lambda zz: start(it, G1, s.g1_send.at[it], s.g1_recv.at[it, lax.div(z, ZS)], to_z(zz)))
-
-        scalar_y(it, [curv_m] if it > 0 else [curv_m, rho_m])
+            each(peers_z, lambda zz: start(it, G1, s.g1_send.at[it], s.g1_recv.at[it, lax.div(z, ZS)], to_z(zz)))
+
+        scalar_y(it, [curv_m])
 
         arrived(it, B2, s.b2_recv.at[it, pl.ds(0, nz - 1)])
         ped = jnp.sum(s.b2_recv[it].astype(F32), axis=0)
         g_row = jnp.sum(jnp.where(trait_col == y, g, 0.0), axis=0, keepdims=True)
         image = a_diag * z_a + ped + jnp.where(blk == gblk, g_row, 0.0)
-        q_a = image if it == 0 else image + beta_y * q_a
-        sums = scalar_end(it)
-        if it == 0:
-            rho = sums[:, 1:2]
-        alpha = rho / sums[:, 0:1]
+        q_a = image + beta_y * q_a
+        alpha = rho_next / scalar_end(it)[:, 0:1]
         alpha_y = mine(alpha)
         sol_a = sol_a + alpha_y * u
         r_a = r_a - alpha_y * q_a
-        z_a = r_a * a_inv
-
+        return r_a * a_inv, r_a, q_a, u, sol_a, v_u, g_u, alpha, beta, rho_next
+
+    none = jnp.zeros((nb, LANES), F32)
+    held = lax.fori_loop(0, ITERS, iterate, (r_a * a_inv, r_a, none, none, none, none, jnp.zeros((traits, LANES), F32),
+                                             col, col, jnp.ones((traits, 1), F32)))
+    _, r_a, _, _, sol_a, _, _, alpha, beta, _ = held
+    last = ITERS - 1
     s.f_send[0] = sol_a
     s.f_send[1] = r_a
     s.f_recv[y] = s.f_send[...]
-    each(y, ny, lambda yy: push(s.f_send, s.f_recv.at[y], s.once_send.at[1], s.once_recv.at[1], to_y(yy)))
-    gather_wide(it)
+    each(peers_y, lambda yy: push(s.f_send, s.f_recv.at[y], s.once_send.at[1], s.once_recv.at[1], to_y(yy)))
+    gather_wide(last)
     for cut in cuts:
         msol[:, cut] = msol[:, cut] + alpha * s.m[:, cut]
-    gather_end(it)
+    gather_end(last)
     for b, cut in enumerate(cuts):
-        mres[:, cut] = mres[:, cut] - alpha * marker_image(it, b)
+        mres[:, cut] = mres[:, cut] - alpha * marker_image(ITERS, b, beta)
     await_bytes(s.f_recv.at[pl.ds(0, ny - 1)], s.once_recv.at[1])
     for t in range(traits):
         for k in range(nb):
@@ -477,7 +473,7 @@
         r1_send=f32(ITERS, JB, traits, wide), r1_recv=f32(ITERS, NJ, traits, wide),
         r2_send=f32(ITERS, ZB, traits, LANES), r2_recv=f32(ITERS, nz, traits, LANES),
         g1_send=f32(ITERS, traits, LANES), g1_recv=f32(ITERS, ZB, traits, LANES),
-        g2_recv=f32(ITERS, JB, ZB, traits, LANES),
+        g2_recv=f32(ITERS + 1, JB, ZB, traits, LANES),
         sz_send=f32(SUMS, 1, LANES), sz_recv=f32(SUMS, nz, 1, LANES),
         sx_send=f32(SUMS, 1, LANES), sx_recv=f32(SUMS, NJ, 1, LANES),
         sy_send=f32(SUMS, traits, LANES), sy_recv=f32(SUMS, ny, traits, LANES),

time: 112 us -> 115 us (1.027)
  Pallas kernels: 109 us -> 112 us
    pallas_call x1, Pallas kernels: 108 us -> 111 us  [body(): pl.pallas_call(run, out_shape=[jax.ShapeDtypeStruct(a.shape, F32) for a i...]
where the time goes in v3:
time: 115 us; the launch traced here: 114 us
  Pallas kernels  112 us (97%)
  between operations  1.93 us (2%)
    pallas_call x1, Pallas kernels, body(): pl.pallas_call(run, out_shape=[jax.ShapeDtypeStruct(a.shape, F32) for a i...  111 us

profile of v3, /device:TPU:1, one launch (start us, length us, event | category | flops | bytes accessed | tf_op | source)
XLA Modules:
  0.0 114.3 jit_solution(745376938878719452)
XLA Ops:
  1.9 110.7 %shard_map.147 = (f32[4,1024]{1,0:T(4,128)}, f32[4,6272]{1,0:T(4,128)}, f32[4,1024]{1,0:T(4,128)}, f32[4,6272]{1,0:T(4,128)}) custom-call(f32[4,1024]{1,0:T(4,128)} %refs_0_.1, f32[4,6272]{1,0:T(4,128)} %refs_1_.1, f32[8,128]{1,0:T(8,128)} %bitcast.3, f32[6272]{0:T(1024)} %refs_3_.1, f32[6272]{0:T(1024)} %refs_4_.1, bf16[64,6272]{1,0:T(8,128)(2,1)} %refs_5_.1, ...), custom_call_target="tpu_custom_call" | custom-call | tf_op jit(solution)/shard_map/pallas_call | solution.py:490
  112.6 1.7 %shard_map.148 = (f32[4,1024]{1,0:T(4,128)}, f32[4,6272]{1,0:T(4,128)}, f32[4,1024]{1,0:T(4,128)}, f32[4,6272]{1,0:T(4,128)}) custom-call(f32[4,1024]{1,0:T(4,128)} %get-tuple-element.8.refs_0_, f32[4,6272]{1,0:T(4,128)} %get-tuple-element.9.refs_1_, f32[4,1024]{1,0:T(4,128)} %get-tuple-element.10.refs_2_, f32[4,6272]{1,0:T(4,128)} %get-tuple-element.11.refs_3_), custom_call_target="tpu_custom_call" | custom-call | tf_op jit(solution)/shard_map/pallas_call | solution.py:513

commit v4 on v3

--- a/solution.py
+++ b/solution.py
@@ -79,7 +79,8 @@
     each(peers_y, lambda yy: greet(to_y(yy)))
 
     pairs = ((arhs_h, s.arhs), (adiag_h, s.adiag), (mrhs_h, s.mrhs), (mdiag_h, s.mdiag.at[0]), (mscale_h, s.mscale.at[0]),
-             (owner_h, s.owner), (local_h, s.local), (rows_h, s.rows), (geno_h, s.g), (w_h, s.w))
+             (owner_h, s.owner), (local_h, s.local), (rows_h, s.rows),
+             (rows_h, s.row_names.at[0]), (geno_h, s.g), (w_h, s.w))
     gets = [pltpu.make_async_copy(src, dst, s.get.at[k]) for k, (src, dst) in enumerate(pairs)]
     for get in gets:
         get.start()
@@ -115,6 +116,8 @@
         s.id_send[...] = asked.reshape(NJ, slots, LANES).astype(BF16)
         each(peers_j, lambda jj: push(s.id_send.at[jj], s.id_recv.at[j], s.once_send.at[0], s.once_recv.at[0], to_j(jj)))
         s.id_recv[j] = s.id_send[j]
+        s.row_hot[...] = jnp.zeros_like(s.row_hot)
+        s.row_hot[:, :tiles] = (iota((8, tiles), 0) == s.row_names[...]).astype(F32)
         s.table[...] = jnp.zeros_like(s.table)
         s.table[:, :tiles] = hit
         table = s.table[...]
@@ -137,7 +140,7 @@
             mres[:, cut] = s.mrhs[:, cut]
             for ref in (s.x, s.q, s.m, msol):
                 ref[:, cut] = jnp.zeros((traits, wide), F32)
-        s.g2_recv[0] = jnp.zeros(s.g2_recv.shape[1:], F32)
+        s.g2_recv[0] = jnp.zeros(s.g2_recv.shape[1:], BF16)
 
     pl.semaphore_wait(barrier, nz + NJ + ny - 3)
 
@@ -207,7 +210,7 @@
 
     def marker_image(n, b, beta):
         cut = cuts[b]
-        summed = jnp.concatenate([s.g2_recv[n, b, c] for c in range(ZB)], axis=1)
+        summed = jnp.concatenate([s.g2_recv[n, b, c].astype(F32) for c in range(ZB)], axis=1)
         return s.mdiag[:, cut] * s.x[:, cut] + s.mscale[:, cut] * summed + beta * s.q[:, cut]
 
     def iterate(it, held):
@@ -268,24 +271,24 @@
             gets[-1].wait()
 
         arrived(it, A2, s.a2_recv.at[it, pl.ds(0, NJ - 1)])
-        fetched = s.a2_recv[it].reshape(all_slots, LANES)
-        s.fetched[...] = jnp.dot(s.placed[...], fetched, preferred_element_type=F32).reshape(LANES // 8, 8, LANES)
-
-        def four(first):
-            w = s.w[pl.ds(first, 4)]
-            return jnp.concatenate([w[0:2].reshape(2 * LANES, LANES), w[2:4].reshape(2 * LANES, LANES)], axis=1)
+        fetched = jnp.dot(s.placed[...], s.a2_recv[it].reshape(all_slots, LANES), preferred_element_type=F32)
+        blocks = fetched.T
+        zero = jnp.zeros_like(blocks)
+        both = jnp.concatenate([jnp.concatenate([blocks, zero], axis=1), jnp.concatenate([zero, blocks], axis=1)], axis=0)
+        both = both.astype(BF16)
 
         def forward(n, acc):
-            rows = s.fetched[n]
-            for h in (0, 4):
-                a, b, c, d = [jnp.where(sub == s.rows[n * 8 + h + k], rows[h + k:h + k + 1], 0.0) for k in range(4)]
-                left = jnp.concatenate([jnp.concatenate([a, c], axis=1), jnp.concatenate([b, d], axis=1)], axis=0)
-                acc += lax.dot_general(left.astype(BF16), four(n * 8 + h), (((1,), (1,)), ((), ())),
-                                       preferred_element_type=F32)
+            w = s.w[pl.ds(n * 8, 8)]
+            left = jnp.concatenate([w[:4].reshape(4 * LANES, LANES), w[4:].reshape(4 * LANES, LANES)], axis=1)
+            out = jnp.dot(left, both, preferred_element_type=F32)
+            for k in range(8):
+                down, across = k % 4 * LANES, k // 4 * LANES
+                acc = jnp.where(column == n * 8 + k, out[down:down + LANES, across:across + LANES], acc)
             return acc
 
-        acc = lax.fori_loop(0, tiles // 8, forward, jnp.zeros((16, 2 * LANES), F32), unroll=True)
-        v = acc[:8, :LANES] + acc[8:, LANES:]
+        column = iota((LANES, LANES), 1)
+        acc = lax.fori_loop(0, tiles // 8, forward, zero, unroll=2)
+        v = jnp.dot(s.row_hot[...], acc.T, preferred_element_type=F32, precision=lax.Precision.HIGHEST)
 
         arrived(it, Y, s.y_recv.at[it, pl.ds(0, ny - 1)])
         g = jnp.zeros((traits, LANES), F32)
@@ -294,7 +297,7 @@
             g += jnp.where(trait_col == t, s.y_recv[it, t, traits:traits + 1, :], 0.0)
         gb = g[:, :geno].astype(BF16)
         for b, cut in enumerate(cuts):
-            s.r1_send[it, b] = jnp.dot(gb, s.g[:, cut], preferred_element_type=F32)
+            s.r1_send[it, b] = jnp.dot(gb, s.g[:, cut], preferred_element_type=F32).astype(BF16)
 
         def send_r1(jj):
             @pl.when(jj < JB)
@@ -313,6 +316,10 @@
         vb = v.astype(BF16).astype(F32)
         twice = jnp.concatenate([jnp.concatenate([vb, zero], axis=1), jnp.concatenate([zero, vb], axis=1)], axis=0)
         twice = twice.astype(BF16)
+
+        def four(first):
+            w = s.w[pl.ds(first, 4)]
+            return jnp.concatenate([w[0:2].reshape(2 * LANES, LANES), w[2:4].reshape(2 * LANES, LANES)], axis=1)
 
         def backward(n, c):
             rows = jnp.zeros((8, LANES), F32)
@@ -344,7 +351,7 @@
         def _():
             s.r1_recv[it, j] = s.r1_send[it, j]
             arrived(it, R1, s.r1_recv.at[it, pl.ds(0, NJ - 1)])
-            part = jnp.sum(s.r1_recv[it], axis=0)
+            part = jnp.sum(s.r1_recv[it].astype(F32), axis=0)
             for b in range(ZB):
                 s.r2_send[it, b] = part[:, b * LANES:(b + 1) * LANES]
 
@@ -366,7 +373,7 @@
         def _():
             s.r2_recv[it, z] = s.r2_send[it, lax.div(z, ZS)]
             arrived(it, R2, s.r2_recv.at[it, pl.ds(0, nz - 1)])
-            part = jnp.sum(s.r2_recv[it], axis=0)
+            part = jnp.sum(s.r2_recv[it], axis=0).astype(BF16)
             s.g1_send[it] = part
             s.g1_recv[it, lax.div(z, ZS)] = part
             each(peers_z, lambda zz: start(it, G1, s.g1_send.at[it], s.g1_recv.at[it, lax.div(z, ZS)], to_z(zz)))
@@ -386,7 +393,7 @@
 
     none = jnp.zeros((nb, LANES), F32)
     held = lax.fori_loop(0, ITERS, iterate, (r_a * a_inv, r_a, none, none, none, none, jnp.zeros((traits, LANES), F32),
-                                             col, col, jnp.ones((traits, 1), F32)))
+                                             col, col, jnp.ones((traits, 1), F32)), unroll=True)
     _, r_a, _, _, sol_a, _, _, alpha, beta, _ = held
     last = ITERS - 1
     s.f_send[0] = sol_a
@@ -426,7 +433,7 @@
             @pl.when(in_zb)
             def _():
                 gone(R2, s.r2_recv, ZB - 1)
-                gone(G1, s.r2_recv, nz - 1)
+                gone(G1, s.g1_gone, nz - 1)
 
             @pl.when(jnp.logical_not(in_zb))
             def _():
@@ -461,7 +468,7 @@
         w=b16(*tile_weights.shape), g=b16(*genotypes.shape),
         placed=b16(LANES, every), placed_t=b16(every, LANES), table=f32(every, LANES),
         pmat=b16(every, nz * nb), pmat_t=b16(nz * nb, every),
-        fetched=f32(LANES // 8, 8, LANES), back=f32(LANES // 8, 8, LANES),
+        row_names=pltpu.VMEM((1, tiles), I32), row_hot=f32(8, LANES), back=f32(LANES // 8, 8, LANES),
         m=f32(traits, markers), q=f32(traits, markers), x=f32(traits, markers),
         m_inv=f32(1, markers),
         id_send=b16(NJ, slots, LANES), id_recv=b16(NJ, slots, LANES),
@@ -470,15 +477,15 @@
         b1_send=b16(ITERS, NJ, slots, LANES), b1_recv=b16(ITERS, NJ, slots, LANES),
         b2_send=b16(ITERS, nz, nb, LANES), b2_recv=b16(ITERS, nz, nb, LANES),
         y_send=f32(ITERS, 8, LANES), y_recv=f32(ITERS, ny, 8, LANES),
-        r1_send=f32(ITERS, JB, traits, wide), r1_recv=f32(ITERS, NJ, traits, wide),
+        r1_send=b16(ITERS, JB, traits, wide), r1_recv=b16(ITERS, NJ, traits, wide),
         r2_send=f32(ITERS, ZB, traits, LANES), r2_recv=f32(ITERS, nz, traits, LANES),
-        g1_send=f32(ITERS, traits, LANES), g1_recv=f32(ITERS, ZB, traits, LANES),
-        g2_recv=f32(ITERS + 1, JB, ZB, traits, LANES),
+        g1_send=b16(ITERS, traits, LANES), g1_recv=b16(ITERS, ZB, traits, LANES),
+        g2_recv=b16(ITERS + 1, JB, ZB, traits, LANES),
         sz_send=f32(SUMS, 1, LANES), sz_recv=f32(SUMS, nz, 1, LANES),
         sx_send=f32(SUMS, 1, LANES), sx_recv=f32(SUMS, NJ, 1, LANES),
         sy_send=f32(SUMS, traits, LANES), sy_recv=f32(SUMS, ny, traits, LANES),
-        f_send=f32(2, nb, LANES), f_recv=f32(ny, 2, nb, LANES),
-        get=dma((10,)), once_send=dma((2,)), once_recv=dma((2,)),
+        g1_gone=b16(ITERS, nz, traits, LANES), f_send=f32(2, nb, LANES), f_recv=f32(ny, 2, nb, LANES),
+        get=dma((11,)), once_send=dma((2,)), once_recv=dma((2,)),
         send=dma((ITERS, STAGES)), recv=dma((ITERS, STAGES)),
         sum_send=dma((SUMS, STEPS)), sum_recv=dma((SUMS, STEPS)),
     )

time: 115 us -> 115 us (level)
  no operation moved by 1% of the time
where the time goes in v4:
time: 115 us
  Pallas kernels  113 us (98%)
  between operations  1.93 us (2%)
    pallas_call x1, Pallas kernels, body(): pl.pallas_call(run, out_shape=[jax.ShapeDtypeStruct(a.shape, F32) for a i...  111 us

profile of v4, /device:TPU:1, one launch (start us, length us, event | category | flops | bytes accessed | tf_op | source)
XLA Modules:
  0.0 114.5 jit_solution(1550896755690709492)
XLA Ops:
  1.9 110.9 %shard_map.147 = (f32[4,1024]{1,0:T(4,128)}, f32[4,6272]{1,0:T(4,128)}, f32[4,1024]{1,0:T(4,128)}, f32[4,6272]{1,0:T(4,128)}) custom-call(f32[4,1024]{1,0:T(4,128)} %refs_0_.1, f32[4,6272]{1,0:T(4,128)} %refs_1_.1, f32[8,128]{1,0:T(8,128)} %bitcast.3, f32[6272]{0:T(1024)} %refs_3_.1, f32[6272]{0:T(1024)} %refs_4_.1, bf16[64,6272]{1,0:T(8,128)(2,1)} %refs_5_.1, ...), custom_call_target="tpu_custom_call" | custom-call | tf_op jit(solution)/shard_map/pallas_call | solution.py:497
  112.8 1.7 %shard_map.148 = (f32[4,1024]{1,0:T(4,128)}, f32[4,6272]{1,0:T(4,128)}, f32[4,1024]{1,0:T(4,128)}, f32[4,6272]{1,0:T(4,128)}) custom-call(f32[4,1024]{1,0:T(4,128)} %get-tuple-element.8.refs_0_, f32[4,6272]{1,0:T(4,128)} %get-tuple-element.9.refs_1_, f32[4,1024]{1,0:T(4,128)} %get-tuple-element.10.refs_2_, f32[4,6272]{1,0:T(4,128)} %get-tuple-element.11.refs_3_), custom_call_target="tpu_custom_call" | custom-call | tf_op jit(solution)/shard_map/pallas_call | solution.py:520

commit v5 on v3

--- a/solution.py
+++ b/solution.py
@@ -14,7 +14,6 @@
 LANES = 128
 A1, A2, B1, B2, Y, R1, R2, G1, G2, STAGES = range(10)
 SZ, SX, SY, STEPS = range(4)
-SUMS = 2 * ITERS
 ANIMALS, SNPS = "animals", "snps"
 MESH = pl.DeviceIdType.MESH
 F32, BF16, I32 = jnp.float32, jnp.bfloat16, jnp.int32
@@ -137,7 +136,7 @@
             mres[:, cut] = s.mrhs[:, cut]
             for ref in (s.x, s.q, s.m, msol):
                 ref[:, cut] = jnp.zeros((traits, wide), F32)
-        s.g2_recv[0] = jnp.zeros(s.g2_recv.shape[1:], F32)
+        s.g2_recv[0] = jnp.zeros(s.g2_recv.shape[1:], BF16)
 
     pl.semaphore_wait(barrier, nz + NJ + ny - 3)
 
@@ -205,19 +204,24 @@
         def _():
             arrived(it, G2, s.g2_recv.at[it + 1])
 
-    def marker_image(n, b, beta):
+    def marker_step(n, b, alpha, beta):
         cut = cuts[b]
-        summed = jnp.concatenate([s.g2_recv[n, b, c] for c in range(ZB)], axis=1)
-        return s.mdiag[:, cut] * s.x[:, cut] + s.mscale[:, cut] * summed + beta * s.q[:, cut]
+        m = s.x[:, cut] + beta * s.m[:, cut]
+        s.m[:, cut] = m
+        msol[:, cut] = msol[:, cut] + alpha * m
+        summed = jnp.concatenate([s.g2_recv[n, b, c].astype(F32) for c in range(ZB)], axis=1)
+        q_m = s.mdiag[:, cut] * s.x[:, cut] + s.mscale[:, cut] * summed + beta * s.q[:, cut]
+        s.q[:, cut] = q_m
+        r_m = mres[:, cut] - alpha * q_m
+        mres[:, cut] = r_m
+        return cut, q_m, r_m
 
     def iterate(it, held):
-        z_a, r_a, q_a, u, sol_a, v_u, g_u, alpha, beta, rho = held
-        norm = ITERS + it
+        z_a, r_a, q_a, u, sol_a, alpha, beta, rho, curv = held
 
         s.a1_send[it] = z_a.astype(BF16)
         s.a1_recv[it, z] = s.a1_send[it]
         each(peers_z, lambda zz: start(it, A1, s.a1_send.at[it], s.a1_recv.at[it, z], to_z(zz)))
-        scalar_z(norm, [r_a * z_a])
 
         @pl.when(it == 0)
         def _():
@@ -238,21 +242,18 @@
         s.a2_recv[it, j] = s.a2_send[it, j]
         each(peers_j, lambda jj: start(it, A2, s.a2_send.at[it, jj], s.a2_recv.at[it, j], to_j(jj)))
 
-        scalar_x(norm)
-
         @pl.when(it > 0)
         def _():
             gather_end(it - 1)
 
-        dot_m, curv_m, rho_m = jnp.zeros((traits, geno), F32), col, col
-        for b, cut in enumerate(cuts):
-            q_m = marker_image(it, b, beta)
-            r_m = mres[:, cut] - alpha * q_m
+        dot_m, rho_m, eta_m, delta_m = jnp.zeros((traits, geno), F32), col, col, col
+        for b in range(JB):
+            cut, q_m, r_m = marker_step(it, b, alpha, beta)
             x_m = r_m * s.m_inv[:, cut]
-            s.q[:, cut] = q_m
-            mres[:, cut] = r_m
             s.x[:, cut] = x_m
             rho_m += jnp.sum(r_m * x_m, axis=1, keepdims=True)
+            eta_m += jnp.sum(q_m * x_m, axis=1, keepdims=True)
+            delta_m += jnp.sum(s.mdiag[:, cut] * x_m * x_m, axis=1, keepdims=True)
             mb = (x_m * s.mscale[:, cut]).astype(BF16)
             dot_m += lax.dot_general(mb, s.g[:, cut], (((1,), (1,)), ((), ())), preferred_element_type=F32)
         own_rows = jnp.sum(jnp.where((blk == gblk) & (lane < geno), z_a, 0.0), axis=0, keepdims=True)
@@ -261,7 +262,6 @@
         s.y_recv[it, y] = s.y_send[it]
         each(peers_y, lambda yy: start(it, Y, s.y_send.at[it], s.y_recv.at[it, y], to_y(yy)))
 
-        scalar_y(norm, [rho_m])
 
         @pl.when(it == 0)
         def _():
@@ -284,7 +284,7 @@
                                        preferred_element_type=F32)
             return acc
 
-        acc = lax.fori_loop(0, tiles // 8, forward, jnp.zeros((16, 2 * LANES), F32), unroll=True)
+        acc = lax.fori_loop(0, tiles // 8, forward, jnp.zeros((16, 2 * LANES), F32), unroll=7)
         v = acc[:8, :LANES] + acc[8:, LANES:]
 
         arrived(it, Y, s.y_recv.at[it, pl.ds(0, ny - 1)])
@@ -294,7 +294,7 @@
             g += jnp.where(trait_col == t, s.y_recv[it, t, traits:traits + 1, :], 0.0)
         gb = g[:, :geno].astype(BF16)
         for b, cut in enumerate(cuts):
-            s.r1_send[it, b] = jnp.dot(gb, s.g[:, cut], preferred_element_type=F32)
+            s.r1_send[it, b] = jnp.dot(gb, s.g[:, cut], preferred_element_type=F32).astype(BF16)
 
         def send_r1(jj):
             @pl.when(jj < JB)
@@ -302,12 +302,9 @@
                 start(it, R1, s.r1_send.at[it, jj], s.r1_recv.at[it, j], to_j(jj))
 
         each(peers_j, send_r1)
-        rho_next = scalar_end(norm)[:, 0:1]
-        beta = jnp.where(it == 0, 0.0, rho_next / rho)
-        beta_y = mine(beta)
-        u, v_u, g_u = z_a + beta_y * u, v + beta_y * v_u, g + beta * g_u
-        g_row = jnp.sum(jnp.where(trait_col == y, g_u, 0.0), axis=0, keepdims=True)
-        scalar_z(it, [a_diag * u * u + v_u * v_u + jnp.where(sub == 0, g_row * g_row, 0.0)])
+        g_row = jnp.sum(jnp.where(trait_col == y, g, 0.0), axis=0, keepdims=True)
+        delta_a = a_diag * z_a * z_a + v * v + jnp.where(sub == 0, g_row * g_row, 0.0)
+        scalar_z(it, [r_a * z_a, z_a * q_a, delta_a])
 
         zero = jnp.zeros((8, LANES), F32)
         vb = v.astype(BF16).astype(F32)
@@ -326,25 +323,18 @@
             s.back[n] = rows
             return c
 
-        lax.fori_loop(0, tiles // 8, backward, 0, unroll=True)
+        lax.fori_loop(0, tiles // 8, backward, 0, unroll=7)
         back = s.back[...].reshape(LANES, LANES).astype(BF16)
         outgoing = jnp.dot(s.placed_t[...], back, preferred_element_type=F32)
         s.b1_send[it] = outgoing.reshape(NJ, slots, LANES).astype(BF16)
         s.b1_recv[it, j] = s.b1_send[it, j]
         each(peers_j, lambda jj: start(it, B1, s.b1_send.at[it, jj], s.b1_recv.at[it, j], to_j(jj)))
 
-        for cut in cuts:
-            m = s.m[:, cut]
-            msol[:, cut] = msol[:, cut] + alpha * m
-            m = s.x[:, cut] + beta * m
-            s.m[:, cut] = m
-            curv_m += jnp.sum(s.mdiag[:, cut] * m * m, axis=1, keepdims=True)
-
         @pl.when(in_jb)
         def _():
             s.r1_recv[it, j] = s.r1_send[it, j]
             arrived(it, R1, s.r1_recv.at[it, pl.ds(0, NJ - 1)])
-            part = jnp.sum(s.r1_recv[it], axis=0)
+            part = jnp.sum(s.r1_recv[it].astype(F32), axis=0)
             for b in range(ZB):
                 s.r2_send[it, b] = part[:, b * LANES:(b + 1) * LANES]
 
@@ -366,39 +356,41 @@
         def _():
             s.r2_recv[it, z] = s.r2_send[it, lax.div(z, ZS)]
             arrived(it, R2, s.r2_recv.at[it, pl.ds(0, nz - 1)])
-            part = jnp.sum(s.r2_recv[it], axis=0)
+            part = jnp.sum(s.r2_recv[it], axis=0).astype(BF16)
             s.g1_send[it] = part
             s.g1_recv[it, lax.div(z, ZS)] = part
             each(peers_z, lambda zz: start(it, G1, s.g1_send.at[it], s.g1_recv.at[it, lax.div(z, ZS)], to_z(zz)))
 
-        scalar_y(it, [curv_m])
+        scalar_y(it, [rho_m, eta_m, delta_m])
 
         arrived(it, B2, s.b2_recv.at[it, pl.ds(0, nz - 1)])
         ped = jnp.sum(s.b2_recv[it].astype(F32), axis=0)
-        g_row = jnp.sum(jnp.where(trait_col == y, g, 0.0), axis=0, keepdims=True)
         image = a_diag * z_a + ped + jnp.where(blk == gblk, g_row, 0.0)
+        sums = scalar_end(it)
+        rho_next = sums[:, 0:1]
+        beta = jnp.where(it == 0, 0.0, rho_next / rho)
+        curv = sums[:, 2:3] + 2.0 * beta * sums[:, 1:2] + beta * beta * curv
+        alpha = rho_next / curv
+        alpha_y, beta_y = mine(alpha), mine(beta)
+        u = z_a + beta_y * u
         q_a = image + beta_y * q_a
-        alpha = rho_next / scalar_end(it)[:, 0:1]
-        alpha_y = mine(alpha)
         sol_a = sol_a + alpha_y * u
         r_a = r_a - alpha_y * q_a
-        return r_a * a_inv, r_a, q_a, u, sol_a, v_u, g_u, alpha, beta, rho_next
+        return r_a * a_inv, r_a, q_a, u, sol_a, alpha, beta, rho_next, curv
 
     none = jnp.zeros((nb, LANES), F32)
-    held = lax.fori_loop(0, ITERS, iterate, (r_a * a_inv, r_a, none, none, none, none, jnp.zeros((traits, LANES), F32),
-                                             col, col, jnp.ones((traits, 1), F32)))
-    _, r_a, _, _, sol_a, _, _, alpha, beta, _ = held
+    held = lax.fori_loop(0, ITERS, iterate, (r_a * a_inv, r_a, none, none, none, col, col, jnp.ones((traits, 1), F32), col),
+                         unroll=True)
+    _, r_a, _, _, sol_a, alpha, beta, _, _ = held
     last = ITERS - 1
     s.f_send[0] = sol_a
     s.f_send[1] = r_a
     s.f_recv[y] = s.f_send[...]
     each(peers_y, lambda yy: push(s.f_send, s.f_recv.at[y], s.once_send.at[1], s.once_recv.at[1], to_y(yy)))
     gather_wide(last)
-    for cut in cuts:
-        msol[:, cut] = msol[:, cut] + alpha * s.m[:, cut]
     gather_end(last)
-    for b, cut in enumerate(cuts):
-        mres[:, cut] = mres[:, cut] - alpha * marker_image(ITERS, b, beta)
+    for b in range(JB):
+        marker_step(ITERS, b, alpha, beta)
     await_bytes(s.f_recv.at[pl.ds(0, ny - 1)], s.once_recv.at[1])
     for t in range(traits):
         for k in range(nb):
@@ -407,7 +399,7 @@
 
     await_bytes(s.id_recv.at[pl.ds(0, NJ - 1)], s.once_send.at[0])
     await_bytes(s.f_recv.at[pl.ds(0, ny - 1)], s.once_send.at[1])
-    for n in range(SUMS):
+    for n in range(ITERS):
         for step, ref, count in ((SZ, s.sz_recv, nz - 1), (SX, s.sx_recv, NJ - 1), (SY, s.sy_recv, ny - 1)):
             await_bytes(ref.at[n, pl.ds(0, count)], s.sum_send.at[n, step])
     for it in range(ITERS):
@@ -426,7 +418,7 @@
             @pl.when(in_zb)
             def _():
                 gone(R2, s.r2_recv, ZB - 1)
-                gone(G1, s.r2_recv, nz - 1)
+                gone(G1, s.g1_gone, nz - 1)
 
             @pl.when(jnp.logical_not(in_zb))
             def _():
@@ -470,17 +462,17 @@
         b1_send=b16(ITERS, NJ, slots, LANES), b1_recv=b16(ITERS, NJ, slots, LANES),
         b2_send=b16(ITERS, nz, nb, LANES), b2_recv=b16(ITERS, nz, nb, LANES),
         y_send=f32(ITERS, 8, LANES), y_recv=f32(ITERS, ny, 8, LANES),
-        r1_send=f32(ITERS, JB, traits, wide), r1_recv=f32(ITERS, NJ, traits, wide),
+        r1_send=b16(ITERS, JB, traits, wide), r1_recv=b16(ITERS, NJ, traits, wide),
         r2_send=f32(ITERS, ZB, traits, LANES), r2_recv=f32(ITERS, nz, traits, LANES),
-        g1_send=f32(ITERS, traits, LANES), g1_recv=f32(ITERS, ZB, traits, LANES),
-        g2_recv=f32(ITERS + 1, JB, ZB, traits, LANES),
-        sz_send=f32(SUMS, 1, LANES), sz_recv=f32(SUMS, nz, 1, LANES),
-        sx_send=f32(SUMS, 1, LANES), sx_recv=f32(SUMS, NJ, 1, LANES),
-        sy_send=f32(SUMS, traits, LANES), sy_recv=f32(SUMS, ny, traits, LANES),
-        f_send=f32(2, nb, LANES), f_recv=f32(ny, 2, nb, LANES),
+        g1_send=b16(ITERS, traits, LANES), g1_recv=b16(ITERS, ZB, traits, LANES),
+        g2_recv=b16(ITERS + 1, JB, ZB, traits, LANES),
+        sz_send=f32(ITERS, 1, LANES), sz_recv=f32(ITERS, nz, 1, LANES),
+        sx_send=f32(ITERS, 1, LANES), sx_recv=f32(ITERS, NJ, 1, LANES),
+        sy_send=f32(ITERS, traits, LANES), sy_recv=f32(ITERS, ny, traits, LANES),
+        g1_gone=b16(ITERS, nz, traits, LANES), f_send=f32(2, nb, LANES), f_recv=f32(ny, 2, nb, LANES),
         get=dma((10,)), once_send=dma((2,)), once_recv=dma((2,)),
         send=dma((ITERS, STAGES)), recv=dma((ITERS, STAGES)),
-        sum_send=dma((SUMS, STEPS)), sum_recv=dma((SUMS, STEPS)),
+        sum_send=dma((ITERS, STEPS)), sum_recv=dma((ITERS, STEPS)),
     )
 
     def run(*refs):

time: 115 us -> 109 us (0.948)
  Pallas kernels: 112 us -> 107 us
    pallas_call x1, Pallas kernels: 111 us -> 105 us  [body(): pl.pallas_call(run, out_shape=[jax.ShapeDtypeStruct(a.shape, F32) for a i...]
where the time goes in v5:
time: 109 us
  Pallas kernels  107 us (98%)
  between operations  1.93 us (2%)
    pallas_call x1, Pallas kernels, body(): pl.pallas_call(run, out_shape=[jax.ShapeDtypeStruct(a.shape, F32) for a i...  105 us

profile of v5, /device:TPU:1, one launch (start us, length us, event | category | flops | bytes accessed | tf_op | source)
XLA Modules:
  0.0 109.1 jit_solution(7182771733573719992)
XLA Ops:
  1.9 105.5 %shard_map.147 = (f32[4,1024]{1,0:T(4,128)}, f32[4,6272]{1,0:T(4,128)}, f32[4,1024]{1,0:T(4,128)}, f32[4,6272]{1,0:T(4,128)}) custom-call(f32[4,1024]{1,0:T(4,128)} %refs_0_.1, f32[4,6272]{1,0:T(4,128)} %refs_1_.1, f32[8,128]{1,0:T(8,128)} %bitcast.3, f32[6272]{0:T(1024)} %refs_3_.1, f32[6272]{0:T(1024)} %refs_4_.1, bf16[64,6272]{1,0:T(8,128)(2,1)} %refs_5_.1, ...), custom_call_target="tpu_custom_call" | custom-call | tf_op jit(solution)/shard_map/pallas_call | solution.py:482
  107.4 1.7 %shard_map.148 = (f32[4,1024]{1,0:T(4,128)}, f32[4,6272]{1,0:T(4,128)}, f32[4,1024]{1,0:T(4,128)}, f32[4,6272]{1,0:T(4,128)}) custom-call(f32[4,1024]{1,0:T(4,128)} %get-tuple-element.8.refs_0_, f32[4,6272]{1,0:T(4,128)} %get-tuple-element.9.refs_1_, f32[4,1024]{1,0:T(4,128)} %get-tuple-element.10.refs_2_, f32[4,6272]{1,0:T(4,128)} %get-tuple-element.11.refs_3_), custom_call_target="tpu_custom_call" | custom-call | tf_op jit(solution)/shard_map/pallas_call | solution.py:505

commit v6 on v5

--- a/solution.py
+++ b/solution.py
@@ -152,7 +152,7 @@
     def scalar_z(n, parts):
         row = jnp.zeros((1, LANES), F32)
         for k, part in enumerate(parts):
-            row = jnp.where(lane4[:1] == k, total(part), row)
+            row = jnp.where(lane4[:1] == k, part, row)
         s.sz_send[n] = row
         s.sz_recv[n, z] = row
         each(peers_z, lambda zz: scalar_push(n, SZ, s.sz_send.at[n], s.sz_recv.at[n, z], to_z(zz)))
@@ -263,6 +263,24 @@
         each(peers_y, lambda yy: start(it, Y, s.y_send.at[it], s.y_recv.at[it, y], to_y(yy)))
 
 
+        arrived(it, Y, s.y_recv.at[it, pl.ds(0, ny - 1)])
+        g = jnp.zeros((traits, LANES), F32)
+        for t in range(ny):
+            g += s.y_recv[it, t, :traits, :]
+            g += jnp.where(trait_col == t, s.y_recv[it, t, traits:traits + 1, :], 0.0)
+        gb = g[:, :geno].astype(BF16)
+        for b, cut in enumerate(cuts):
+            s.r1_send[it, b] = jnp.dot(gb, s.g[:, cut], preferred_element_type=F32).astype(BF16)
+
+        def send_r1(jj):
+            @pl.when(jj < JB)
+            def _():
+                start(it, R1, s.r1_send.at[it, jj], s.r1_recv.at[it, j], to_j(jj))
+
+        each(peers_j, send_r1)
+        g_row = jnp.sum(jnp.where(trait_col == y, g, 0.0), axis=0, keepdims=True)
+        known = [total(r_a * z_a), total(z_a * q_a), total(a_diag * z_a * z_a) + total(g_row * g_row)]
+
         @pl.when(it == 0)
         def _():
             gets[-1].wait()
@@ -287,24 +305,7 @@
         acc = lax.fori_loop(0, tiles // 8, forward, jnp.zeros((16, 2 * LANES), F32), unroll=7)
         v = acc[:8, :LANES] + acc[8:, LANES:]
 
-        arrived(it, Y, s.y_recv.at[it, pl.ds(0, ny - 1)])
-        g = jnp.zeros((traits, LANES), F32)
-        for t in range(ny):
-            g += s.y_recv[it, t, :traits, :]
-            g += jnp.where(trait_col == t, s.y_recv[it, t, traits:traits + 1, :], 0.0)
-        gb = g[:, :geno].astype(BF16)
-        for b, cut in enumerate(cuts):
-            s.r1_send[it, b] = jnp.dot(gb, s.g[:, cut], preferred_element_type=F32).astype(BF16)
-
-        def send_r1(jj):
-            @pl.when(jj < JB)
-            def _():
-                start(it, R1, s.r1_send.at[it, jj], s.r1_recv.at[it, j], to_j(jj))
-
-        each(peers_j, send_r1)
-        g_row = jnp.sum(jnp.where(trait_col == y, g, 0.0), axis=0, keepdims=True)
-        delta_a = a_diag * z_a * z_a + v * v + jnp.where(sub == 0, g_row * g_row, 0.0)
-        scalar_z(it, [r_a * z_a, z_a * q_a, delta_a])
+        scalar_z(it, known[:2] + [known[2] + total(v * v)])
 
         zero = jnp.zeros((8, LANES), F32)
         vb = v.astype(BF16).astype(F32)

time: 109 us -> 110 us (level)
  no operation moved by 1% of the time
where the time goes in v6:
time: 110 us
  Pallas kernels  108 us (98%)
  between operations  1.93 us (2%)
    pallas_call x1, Pallas kernels, body(): pl.pallas_call(run, out_shape=[jax.ShapeDtypeStruct(a.shape, F32) for a i...  106 us

profile of v6, /device:TPU:1, one launch (start us, length us, event | category | flops | bytes accessed | tf_op | source)
XLA Modules:
  0.0 109.5 jit_solution(7620140483054092145)
XLA Ops:
  1.9 105.9 %shard_map.147 = (f32[4,1024]{1,0:T(4,128)}, f32[4,6272]{1,0:T(4,128)}, f32[4,1024]{1,0:T(4,128)}, f32[4,6272]{1,0:T(4,128)}) custom-call(f32[4,1024]{1,0:T(4,128)} %refs_0_.1, f32[4,6272]{1,0:T(4,128)} %refs_1_.1, f32[8,128]{1,0:T(8,128)} %bitcast.3, f32[6272]{0:T(1024)} %refs_3_.1, f32[6272]{0:T(1024)} %refs_4_.1, bf16[64,6272]{1,0:T(8,128)(2,1)} %refs_5_.1, ...), custom_call_target="tpu_custom_call" | custom-call | tf_op jit(solution)/shard_map/pallas_call | solution.py:483
  107.8 1.7 %shard_map.148 = (f32[4,1024]{1,0:T(4,128)}, f32[4,6272]{1,0:T(4,128)}, f32[4,1024]{1,0:T(4,128)}, f32[4,6272]{1,0:T(4,128)}) custom-call(f32[4,1024]{1,0:T(4,128)} %get-tuple-element.8.refs_0_, f32[4,6272]{1,0:T(4,128)} %get-tuple-element.9.refs_1_, f32[4,1024]{1,0:T(4,128)} %get-tuple-element.10.refs_2_, f32[4,6272]{1,0:T(4,128)} %get-tuple-element.11.refs_3_), custom_call_target="tpu_custom_call" | custom-call | tf_op jit(solution)/shard_map/pallas_call | solution.py:506

commit v7 on v6

--- a/solution.py
+++ b/solution.py
@@ -78,7 +78,8 @@
     each(peers_y, lambda yy: greet(to_y(yy)))
 
     pairs = ((arhs_h, s.arhs), (adiag_h, s.adiag), (mrhs_h, s.mrhs), (mdiag_h, s.mdiag.at[0]), (mscale_h, s.mscale.at[0]),
-             (owner_h, s.owner), (local_h, s.local), (rows_h, s.rows), (geno_h, s.g), (w_h, s.w))
+             (owner_h, s.owner), (local_h, s.local), (rows_h, s.rows),
+             (rows_h, s.row_names.at[0]), (geno_h, s.g), (w_h, s.w))
     gets = [pltpu.make_async_copy(src, dst, s.get.at[k]) for k, (src, dst) in enumerate(pairs)]
     for get in gets:
         get.start()
@@ -114,6 +115,8 @@
         s.id_send[...] = asked.reshape(NJ, slots, LANES).astype(BF16)
         each(peers_j, lambda jj: push(s.id_send.at[jj], s.id_recv.at[j], s.once_send.at[0], s.once_recv.at[0], to_j(jj)))
         s.id_recv[j] = s.id_send[j]
+        s.row_hot[...] = jnp.zeros_like(s.row_hot)
+        s.row_hot[:, :tiles] = (iota((8, tiles), 0) == s.row_names[...]).astype(F32)
         s.table[...] = jnp.zeros_like(s.table)
         s.table[:, :tiles] = hit
         table = s.table[...]
@@ -262,7 +265,6 @@
         s.y_recv[it, y] = s.y_send[it]
         each(peers_y, lambda yy: start(it, Y, s.y_send.at[it], s.y_recv.at[it, y], to_y(yy)))
 
-
         arrived(it, Y, s.y_recv.at[it, pl.ds(0, ny - 1)])
         g = jnp.zeros((traits, LANES), F32)
         for t in range(ny):
@@ -286,24 +288,25 @@
             gets[-1].wait()
 
         arrived(it, A2, s.a2_recv.at[it, pl.ds(0, NJ - 1)])
-        fetched = s.a2_recv[it].reshape(all_slots, LANES)
-        s.fetched[...] = jnp.dot(s.placed[...], fetched, preferred_element_type=F32).reshape(LANES // 8, 8, LANES)
-
-        def four(first):
-            w = s.w[pl.ds(first, 4)]
-            return jnp.concatenate([w[0:2].reshape(2 * LANES, LANES), w[2:4].reshape(2 * LANES, LANES)], axis=1)
+        fetched = jnp.dot(s.placed[...], s.a2_recv[it].reshape(all_slots, LANES), preferred_element_type=F32)
+        blocks = fetched.T
+        zero = jnp.zeros_like(blocks)
+        both = jnp.concatenate([jnp.concatenate([blocks, zero], axis=1), jnp.concatenate([zero, blocks], axis=1)], axis=0)
+        both = both.astype(BF16)
 
         def forward(n, acc):
-            rows = s.fetched[n]
-            for h in (0, 4):
-                a, b, c, d = [jnp.where(sub == s.rows[n * 8 + h + k], rows[h + k:h + k + 1], 0.0) for k in range(4)]
-                left = jnp.concatenate([jnp.concatenate([a, c], axis=1), jnp.concatenate([b, d], axis=1)], axis=0)
-                acc += lax.dot_general(left.astype(BF16), four(n * 8 + h), (((1,), (1,)), ((), ())),
-                                       preferred_element_type=F32)
+            w = s.w[pl.ds(n * 8, 8)]
+            left = jnp.concatenate([w[:4].reshape(4 * LANES, LANES), w[4:].reshape(4 * LANES, LANES)], axis=1)
+            out = jnp.dot(left, both, preferred_element_type=F32)
+            for k in range(8):
+                down, across = k % 4 * LANES, k // 4 * LANES
+                acc = jnp.where(column == n * 8 + k, out[down:down + LANES, across:across + LANES], acc)
             return acc
 
-        acc = lax.fori_loop(0, tiles // 8, forward, jnp.zeros((16, 2 * LANES), F32), unroll=7)
-        v = acc[:8, :LANES] + acc[8:, LANES:]
+        column = iota((LANES, LANES), 1)
+        acc = lax.fori_loop(0, tiles // 8, forward, zero, unroll=2)
+        v = lax.dot_general(s.row_hot[...], acc, (((1,), (1,)), ((), ())), preferred_element_type=F32,
+                            precision=lax.Precision.HIGHEST)
 
         scalar_z(it, known[:2] + [known[2] + total(v * v)])
 
@@ -311,6 +314,10 @@
         vb = v.astype(BF16).astype(F32)
         twice = jnp.concatenate([jnp.concatenate([vb, zero], axis=1), jnp.concatenate([zero, vb], axis=1)], axis=0)
         twice = twice.astype(BF16)
+
+        def four(first):
+            w = s.w[pl.ds(first, 4)]
+            return jnp.concatenate([w[0:2].reshape(2 * LANES, LANES), w[2:4].reshape(2 * LANES, LANES)], axis=1)
 
         def backward(n, c):
             rows = jnp.zeros((8, LANES), F32)
@@ -337,7 +344,7 @@
             arrived(it, R1, s.r1_recv.at[it, pl.ds(0, NJ - 1)])
             part = jnp.sum(s.r1_recv[it].astype(F32), axis=0)
             for b in range(ZB):
-                s.r2_send[it, b] = part[:, b * LANES:(b + 1) * LANES]
+                s.r2_send[it, b] = part[:, b * LANES:(b + 1) * LANES].astype(BF16)
 
             for b in range(ZB):
                 @pl.when(b * ZS != z)
@@ -357,7 +364,7 @@
         def _():
             s.r2_recv[it, z] = s.r2_send[it, lax.div(z, ZS)]
             arrived(it, R2, s.r2_recv.at[it, pl.ds(0, nz - 1)])
-            part = jnp.sum(s.r2_recv[it], axis=0).astype(BF16)
+            part = jnp.sum(s.r2_recv[it].astype(F32), axis=0).astype(BF16)
             s.g1_send[it] = part
             s.g1_recv[it, lax.div(z, ZS)] = part
             each(peers_z, lambda zz: start(it, G1, s.g1_send.at[it], s.g1_recv.at[it, lax.div(z, ZS)], to_z(zz)))
@@ -389,17 +396,7 @@
     s.f_recv[y] = s.f_send[...]
     each(peers_y, lambda yy: push(s.f_send, s.f_recv.at[y], s.once_send.at[1], s.once_recv.at[1], to_y(yy)))
     gather_wide(last)
-    gather_end(last)
-    for b in range(JB):
-        marker_step(ITERS, b, alpha, beta)
-    await_bytes(s.f_recv.at[pl.ds(0, ny - 1)], s.once_recv.at[1])
-    for t in range(traits):
-        for k in range(nb):
-            asol[t:t + 1, k * LANES:(k + 1) * LANES] = s.f_recv[t, 0, k:k + 1, :]
-            ares[t:t + 1, k * LANES:(k + 1) * LANES] = s.f_recv[t, 1, k:k + 1, :]
-
     await_bytes(s.id_recv.at[pl.ds(0, NJ - 1)], s.once_send.at[0])
-    await_bytes(s.f_recv.at[pl.ds(0, ny - 1)], s.once_send.at[1])
     for n in range(ITERS):
         for step, ref, count in ((SZ, s.sz_recv, nz - 1), (SX, s.sx_recv, NJ - 1), (SY, s.sy_recv, ny - 1)):
             await_bytes(ref.at[n, pl.ds(0, count)], s.sum_send.at[n, step])
@@ -419,7 +416,7 @@
             @pl.when(in_zb)
             def _():
                 gone(R2, s.r2_recv, ZB - 1)
-                gone(G1, s.g1_gone, nz - 1)
+                gone(G1, s.r2_recv, nz - 1)
 
             @pl.when(jnp.logical_not(in_zb))
             def _():
@@ -428,6 +425,16 @@
         @pl.when(jnp.logical_not(in_jb))
         def _():
             gone(R1, s.r1_recv, JB)
+
+    gather_end(last)
+    for b in range(JB):
+        marker_step(ITERS, b, alpha, beta)
+    await_bytes(s.f_recv.at[pl.ds(0, ny - 1)], s.once_recv.at[1])
+    await_bytes(s.f_recv.at[pl.ds(0, ny - 1)], s.once_send.at[1])
+    for t in range(traits):
+        for k in range(nb):
+            asol[t:t + 1, k * LANES:(k + 1) * LANES] = s.f_recv[t, 0, k:k + 1, :]
+            ares[t:t + 1, k * LANES:(k + 1) * LANES] = s.f_recv[t, 1, k:k + 1, :]
 
 
 def body(animal_rhs, marker_rhs, animal_diagonal, marker_diagonal, marker_scale, genotypes, tile_weights,
@@ -454,7 +461,7 @@
         w=b16(*tile_weights.shape), g=b16(*genotypes.shape),
         placed=b16(LANES, every), placed_t=b16(every, LANES), table=f32(every, LANES),
         pmat=b16(every, nz * nb), pmat_t=b16(nz * nb, every),
-        fetched=f32(LANES // 8, 8, LANES), back=f32(LANES // 8, 8, LANES),
+        row_names=pltpu.VMEM((1, tiles), I32), row_hot=f32(8, LANES), back=f32(LANES // 8, 8, LANES),
         m=f32(traits, markers), q=f32(traits, markers), x=f32(traits, markers),
         m_inv=f32(1, markers),
         id_send=b16(NJ, slots, LANES), id_recv=b16(NJ, slots, LANES),
@@ -464,14 +471,14 @@
         b2_send=b16(ITERS, nz, nb, LANES), b2_recv=b16(ITERS, nz, nb, LANES),
         y_send=f32(ITERS, 8, LANES), y_recv=f32(ITERS, ny, 8, LANES),
         r1_send=b16(ITERS, JB, traits, wide), r1_recv=b16(ITERS, NJ, traits, wide),
-        r2_send=f32(ITERS, ZB, traits, LANES), r2_recv=f32(ITERS, nz, traits, LANES),
+        r2_send=b16(ITERS, ZB, traits, LANES), r2_recv=b16(ITERS, nz, traits, LANES),
         g1_send=b16(ITERS, traits, LANES), g1_recv=b16(ITERS, ZB, traits, LANES),
         g2_recv=b16(ITERS + 1, JB, ZB, traits, LANES),
         sz_send=f32(ITERS, 1, LANES), sz_recv=f32(ITERS, nz, 1, LANES),
         sx_send=f32(ITERS, 1, LANES), sx_recv=f32(ITERS, NJ, 1, LANES),
         sy_send=f32(ITERS, traits, LANES), sy_recv=f32(ITERS, ny, traits, LANES),
-        g1_gone=b16(ITERS, nz, traits, LANES), f_send=f32(2, nb, LANES), f_recv=f32(ny, 2, nb, LANES),
-        get=dma((10,)), once_send=dma((2,)), once_recv=dma((2,)),
+        f_send=f32(2, nb, LANES), f_recv=f32(ny, 2, nb, LANES),
+        get=dma((11,)), once_send=dma((2,)), once_recv=dma((2,)),
         send=dma((ITERS, STAGES)), recv=dma((ITERS, STAGES)),
         sum_send=dma((ITERS, STEPS)), sum_recv=dma((ITERS, STEPS)),
     )

time: 110 us -> 112 us (1.018)
  Pallas kernels: 108 us -> 110 us
    pallas_call x1, Pallas kernels: 106 us -> 108 us  [body(): pl.pallas_call(run, out_shape=[jax.ShapeDtypeStruct(a.shape, F32) for a i...]
where the time goes in v7:
time: 112 us
  Pallas kernels  110 us (98%)
  between operations  1.93 us (2%)
    pallas_call x1, Pallas kernels, body(): pl.pallas_call(run, out_shape=[jax.ShapeDtypeStruct(a.shape, F32) for a i...  108 us

profile of v7, /device:TPU:1, one launch (start us, length us, event | category | flops | bytes accessed | tf_op | source)
XLA Modules:
  0.0 112.0 jit_solution(14392204033286146007)
XLA Ops:
  1.9 108.4 %shard_map.147 = (f32[4,1024]{1,0:T(4,128)}, f32[4,6272]{1,0:T(4,128)}, f32[4,1024]{1,0:T(4,128)}, f32[4,6272]{1,0:T(4,128)}) custom-call(f32[4,1024]{1,0:T(4,128)} %refs_0_.1, f32[4,6272]{1,0:T(4,128)} %refs_1_.1, f32[8,128]{1,0:T(8,128)} %bitcast.3, f32[6272]{0:T(1024)} %refs_3_.1, f32[6272]{0:T(1024)} %refs_4_.1, bf16[64,6272]{1,0:T(8,128)(2,1)} %refs_5_.1, ...), custom_call_target="tpu_custom_call" | custom-call | tf_op jit(solution)/shard_map/pallas_call | solution.py:490
  110.3 1.7 %shard_map.148 = (f32[4,1024]{1,0:T(4,128)}, f32[4,6272]{1,0:T(4,128)}, f32[4,1024]{1,0:T(4,128)}, f32[4,6272]{1,0:T(4,128)}) custom-call(f32[4,1024]{1,0:T(4,128)} %get-tuple-element.8.refs_0_, f32[4,6272]{1,0:T(4,128)} %get-tuple-element.9.refs_1_, f32[4,1024]{1,0:T(4,128)} %get-tuple-element.10.refs_2_, f32[4,6272]{1,0:T(4,128)} %get-tuple-element.11.refs_3_), custom_call_target="tpu_custom_call" | custom-call | tf_op jit(solution)/shard_map/pallas_call | solution.py:513

commit v8 on v6

--- a/solution.py
+++ b/solution.py
@@ -262,7 +262,6 @@
         s.y_recv[it, y] = s.y_send[it]
         each(peers_y, lambda yy: start(it, Y, s.y_send.at[it], s.y_recv.at[it, y], to_y(yy)))
 
-
         arrived(it, Y, s.y_recv.at[it, pl.ds(0, ny - 1)])
         g = jnp.zeros((traits, LANES), F32)
         for t in range(ny):
@@ -302,7 +301,7 @@
                                        preferred_element_type=F32)
             return acc
 
-        acc = lax.fori_loop(0, tiles // 8, forward, jnp.zeros((16, 2 * LANES), F32), unroll=7)
+        acc = lax.fori_loop(0, tiles // 8, forward, jnp.zeros((16, 2 * LANES), F32), unroll=True)
         v = acc[:8, :LANES] + acc[8:, LANES:]
 
         scalar_z(it, known[:2] + [known[2] + total(v * v)])
@@ -324,7 +323,7 @@
             s.back[n] = rows
             return c
 
-        lax.fori_loop(0, tiles // 8, backward, 0, unroll=7)
+        lax.fori_loop(0, tiles // 8, backward, 0, unroll=True)
         back = s.back[...].reshape(LANES, LANES).astype(BF16)
         outgoing = jnp.dot(s.placed_t[...], back, preferred_element_type=F32)
         s.b1_send[it] = outgoing.reshape(NJ, slots, LANES).astype(BF16)
@@ -337,7 +336,7 @@
             arrived(it, R1, s.r1_recv.at[it, pl.ds(0, NJ - 1)])
             part = jnp.sum(s.r1_recv[it].astype(F32), axis=0)
             for b in range(ZB):
-                s.r2_send[it, b] = part[:, b * LANES:(b + 1) * LANES]
+                s.r2_send[it, b] = part[:, b * LANES:(b + 1) * LANES].astype(BF16)
 
             for b in range(ZB):
                 @pl.when(b * ZS != z)
@@ -357,7 +356,7 @@
         def _():
             s.r2_recv[it, z] = s.r2_send[it, lax.div(z, ZS)]
             arrived(it, R2, s.r2_recv.at[it, pl.ds(0, nz - 1)])
-            part = jnp.sum(s.r2_recv[it], axis=0).astype(BF16)
+            part = jnp.sum(s.r2_recv[it].astype(F32), axis=0).astype(BF16)
             s.g1_send[it] = part
             s.g1_recv[it, lax.div(z, ZS)] = part
             each(peers_z, lambda zz: start(it, G1, s.g1_send.at[it], s.g1_recv.at[it, lax.div(z, ZS)], to_z(zz)))
@@ -389,17 +388,7 @@
     s.f_recv[y] = s.f_send[...]
     each(peers_y, lambda yy: push(s.f_send, s.f_recv.at[y], s.once_send.at[1], s.once_recv.at[1], to_y(yy)))
     gather_wide(last)
-    gather_end(last)
-    for b in range(JB):
-        marker_step(ITERS, b, alpha, beta)
-    await_bytes(s.f_recv.at[pl.ds(0, ny - 1)], s.once_recv.at[1])
-    for t in range(traits):
-        for k in range(nb):
-            asol[t:t + 1, k * LANES:(k + 1) * LANES] = s.f_recv[t, 0, k:k + 1, :]
-            ares[t:t + 1, k * LANES:(k + 1) * LANES] = s.f_recv[t, 1, k:k + 1, :]
-
     await_bytes(s.id_recv.at[pl.ds(0, NJ - 1)], s.once_send.at[0])
-    await_bytes(s.f_recv.at[pl.ds(0, ny - 1)], s.once_send.at[1])
     for n in range(ITERS):
         for step, ref, count in ((SZ, s.sz_recv, nz - 1), (SX, s.sx_recv, NJ - 1), (SY, s.sy_recv, ny - 1)):
             await_bytes(ref.at[n, pl.ds(0, count)], s.sum_send.at[n, step])
@@ -419,7 +408,7 @@
             @pl.when(in_zb)
             def _():
                 gone(R2, s.r2_recv, ZB - 1)
-                gone(G1, s.g1_gone, nz - 1)
+                gone(G1, s.r2_recv, nz - 1)
 
             @pl.when(jnp.logical_not(in_zb))
             def _():
@@ -428,6 +417,16 @@
         @pl.when(jnp.logical_not(in_jb))
         def _():
             gone(R1, s.r1_recv, JB)
+
+    gather_end(last)
+    for b in range(JB):
+        marker_step(ITERS, b, alpha, beta)
+    await_bytes(s.f_recv.at[pl.ds(0, ny - 1)], s.once_recv.at[1])
+    await_bytes(s.f_recv.at[pl.ds(0, ny - 1)], s.once_send.at[1])
+    for t in range(traits):
+        for k in range(nb):
+            asol[t:t + 1, k * LANES:(k + 1) * LANES] = s.f_recv[t, 0, k:k + 1, :]
+            ares[t:t + 1, k * LANES:(k + 1) * LANES] = s.f_recv[t, 1, k:k + 1, :]
 
 
 def body(animal_rhs, marker_rhs, animal_diagonal, marker_diagonal, marker_scale, genotypes, tile_weights,
@@ -464,13 +463,13 @@
         b2_send=b16(ITERS, nz, nb, LANES), b2_recv=b16(ITERS, nz, nb, LANES),
         y_send=f32(ITERS, 8, LANES), y_recv=f32(ITERS, ny, 8, LANES),
         r1_send=b16(ITERS, JB, traits, wide), r1_recv=b16(ITERS, NJ, traits, wide),
-        r2_send=f32(ITERS, ZB, traits, LANES), r2_recv=f32(ITERS, nz, traits, LANES),
+        r2_send=b16(ITERS, ZB, traits, LANES), r2_recv=b16(ITERS, nz, traits, LANES),
         g1_send=b16(ITERS, traits, LANES), g1_recv=b16(ITERS, ZB, traits, LANES),
         g2_recv=b16(ITERS + 1, JB, ZB, traits, LANES),
         sz_send=f32(ITERS, 1, LANES), sz_recv=f32(ITERS, nz, 1, LANES),
         sx_send=f32(ITERS, 1, LANES), sx_recv=f32(ITERS, NJ, 1, LANES),
         sy_send=f32(ITERS, traits, LANES), sy_recv=f32(ITERS, ny, traits, LANES),
-        g1_gone=b16(ITERS, nz, traits, LANES), f_send=f32(2, nb, LANES), f_recv=f32(ny, 2, nb, LANES),
+        f_send=f32(2, nb, LANES), f_recv=f32(ny, 2, nb, LANES),
         get=dma((10,)), once_send=dma((2,)), once_recv=dma((2,)),
         send=dma((ITERS, STAGES)), recv=dma((ITERS, STAGES)),
         sum_send=dma((ITERS, STEPS)), sum_recv=dma((ITERS, STEPS)),

time: 110 us -> 111 us (level)
  no operation moved by 1% of the time
where the time goes in v8:
time: 111 us
  Pallas kernels  109 us (98%)
  between operations  1.93 us (2%)
    pallas_call x1, Pallas kernels, body(): pl.pallas_call(run, out_shape=[jax.ShapeDtypeStruct(a.shape, F32) for a i...  107 us

profile of v8, /device:TPU:1, one launch (start us, length us, event | category | flops | bytes accessed | tf_op | source)
XLA Modules:
  0.0 110.6 jit_solution(4788036696897645514)
XLA Ops:
  1.9 106.9 %shard_map.147 = (f32[4,1024]{1,0:T(4,128)}, f32[4,6272]{1,0:T(4,128)}, f32[4,1024]{1,0:T(4,128)}, f32[4,6272]{1,0:T(4,128)}) custom-call(f32[4,1024]{1,0:T(4,128)} %refs_0_.1, f32[4,6272]{1,0:T(4,128)} %refs_1_.1, f32[8,128]{1,0:T(8,128)} %bitcast.3, f32[6272]{0:T(1024)} %refs_3_.1, f32[6272]{0:T(1024)} %refs_4_.1, bf16[64,6272]{1,0:T(8,128)(2,1)} %refs_5_.1, ...), custom_call_target="tpu_custom_call" | custom-call | tf_op jit(solution)/shard_map/pallas_call | solution.py:482
  108.9 1.7 %shard_map.148 = (f32[4,1024]{1,0:T(4,128)}, f32[4,6272]{1,0:T(4,128)}, f32[4,1024]{1,0:T(4,128)}, f32[4,6272]{1,0:T(4,128)}) custom-call(f32[4,1024]{1,0:T(4,128)} %get-tuple-element.8.refs_0_, f32[4,6272]{1,0:T(4,128)} %get-tuple-element.9.refs_1_, f32[4,1024]{1,0:T(4,128)} %get-tuple-element.10.refs_2_, f32[4,6272]{1,0:T(4,128)} %get-tuple-element.11.refs_3_), custom_call_target="tpu_custom_call" | custom-call | tf_op jit(solution)/shard_map/pallas_call | solution.py:505

commit v9 on v8

--- a/solution.py
+++ b/solution.py
@@ -301,7 +301,7 @@
                                        preferred_element_type=F32)
             return acc
 
-        acc = lax.fori_loop(0, tiles // 8, forward, jnp.zeros((16, 2 * LANES), F32), unroll=True)
+        acc = lax.fori_loop(0, tiles // 8, forward, jnp.zeros((16, 2 * LANES), F32), unroll=2)
         v = acc[:8, :LANES] + acc[8:, LANES:]
 
         scalar_z(it, known[:2] + [known[2] + total(v * v)])
@@ -323,7 +323,7 @@
             s.back[n] = rows
             return c
 
-        lax.fori_loop(0, tiles // 8, backward, 0, unroll=True)
+        lax.fori_loop(0, tiles // 8, backward, 0, unroll=2)
         back = s.back[...].reshape(LANES, LANES).astype(BF16)
         outgoing = jnp.dot(s.placed_t[...], back, preferred_element_type=F32)
         s.b1_send[it] = outgoing.reshape(NJ, slots, LANES).astype(BF16)

time: 111 us -> 111 us (level)
  no operation moved by 1% of the time
where the time goes in v9:
time: 111 us
  Pallas kernels  109 us (98%)
  between operations  1.93 us (2%)
    pallas_call x1, Pallas kernels, body(): pl.pallas_call(run, out_shape=[jax.ShapeDtypeStruct(a.shape, F32) for a i...  107 us

profile of v9, /device:TPU:1, one launch (start us, length us, event | category | flops | bytes accessed | tf_op | source)
XLA Modules:
  0.0 110.6 jit_solution(9159889421232566684)
XLA Ops:
  1.9 107.0 %shard_map.147 = (f32[4,1024]{1,0:T(4,128)}, f32[4,6272]{1,0:T(4,128)}, f32[4,1024]{1,0:T(4,128)}, f32[4,6272]{1,0:T(4,128)}) custom-call(f32[4,1024]{1,0:T(4,128)} %refs_0_.1, f32[4,6272]{1,0:T(4,128)} %refs_1_.1, f32[8,128]{1,0:T(8,128)} %bitcast.3, f32[6272]{0:T(1024)} %refs_3_.1, f32[6272]{0:T(1024)} %refs_4_.1, bf16[64,6272]{1,0:T(8,128)(2,1)} %refs_5_.1, ...), custom_call_target="tpu_custom_call" | custom-call | tf_op jit(solution)/shard_map/pallas_call | solution.py:482
  108.9 1.7 %shard_map.148 = (f32[4,1024]{1,0:T(4,128)}, f32[4,6272]{1,0:T(4,128)}, f32[4,1024]{1,0:T(4,128)}, f32[4,6272]{1,0:T(4,128)}) custom-call(f32[4,1024]{1,0:T(4,128)} %get-tuple-element.8.refs_0_, f32[4,6272]{1,0:T(4,128)} %get-tuple-element.9.refs_1_, f32[4,1024]{1,0:T(4,128)} %get-tuple-element.10.refs_2_, f32[4,6272]{1,0:T(4,128)} %get-tuple-element.11.refs_3_), custom_call_target="tpu_custom_call" | custom-call | tf_op jit(solution)/shard_map/pallas_call | solution.py:505
